TPU v7x, 32 devices: a whole 2x2x4 slice. The times are simulated.
32 devices in a mesh: wide: 8 (over y, x, core), narrow: 4 (over z).
Axes of the slice: x: 2, y: 2, z: 4, core: 2. Of those that a mesh axis runs over, the one named last changes fastest.
Arguments:
- block_input: bfloat16 [12288, 768], P('wide', 'narrow'), may hold values from -4 to 4
- time_embed: float32 [24, 128], P('wide'), may hold values from -3 to 3
- seq_lengths: int32 [8, 3], P('wide'), may hold values from 1 to 768, 1536 in all within a row
- w_qkv: bfloat16 [3, 768, 768], P(None, None, 'narrow'), may hold values from -0.21875 to 0.21875
- w_out: bfloat16 [768, 768], P('narrow'), may hold values from -0.625 to 0.625
- w_up: bfloat16 [768, 3072], P(None, 'narrow'), may hold values from -0.21875 to 0.21875
- b_up: float32 [3072], P('narrow'), may hold values from -1.5 to 1.5
- w_down: bfloat16 [3072, 768], P('narrow'), may hold values from -0.109375 to 0.109375
- b_down: float32 [768], replicated, may hold values from -1.5 to 1.5
- gain_one: float32 [768], replicated, may hold values from 0.5 to 1.5
- gain_two: float32 [768], replicated, may hold values from 0.5 to 1.5
- w_ada: bfloat16 [128, 4608], replicated, may hold values from -0.5 to 0.5
- b_ada: float32 [4608], replicated, may hold values from -0.9 to 0.9
- out_grad: bfloat16 [12288, 768], P('wide', 'narrow'), may hold values from -4 to 4
Outputs:
- block_output: bfloat16 [12288, 768], P('wide', 'narrow')
- input_grad: float32 [12288, 768], P('wide', 'narrow')
- time_grad: float32 [24, 128], P('wide')
- grad_qkv: float32 [3, 768, 768], P(None, None, 'narrow')
- grad_out: float32 [768, 768], P('narrow')
- grad_up: float32 [768, 3072], P(None, 'narrow')
- grad_bias_up: float32 [3072], P('narrow')
- grad_down: float32 [3072, 768], P('narrow')
- grad_bias_down: float32 [768], replicated
- grad_gain_one: float32 [768], replicated
- grad_gain_two: float32 [768], replicated
- grad_ada: float32 [128, 4608], replicated
- grad_bias_ada: float32 [4608], replicated
Inputs may be any that keep to these rules, and one draw needn't show every extreme that they name: `seq_lengths`: each row holds the lengths of the 3 sequences of one index of wide, summing to 1536; the largest in each row is exactly 768.
All inputs are finite; a program needn't handle non-finite values.
Results may differ from a plain program's by a relative error of at most 0.023.
The roundings to bfloat16 on the way count: a program that leaves them out, or rounds other values in their place, can miss the bound.
Values may be sent and summed in bfloat16 or wider, within the bound.
A program may use at most 192 MiB of HBM per device.

v0:
```python
import jax
import jax.numpy as jnp
from jax import lax
from jax.sharding import PartitionSpec as P

HD = 64


epsilon = 1e-05
highest = lax.Precision.HIGHEST


def norm_stats(inputs):
    row_mean = jnp.mean(inputs, axis=-1, keepdims=True)
    centered = inputs - row_mean
    variance = jnp.mean(centered * centered, axis=-1, keepdims=True)
    scaled = lax.rsqrt(variance + epsilon)
    return (centered * scaled, scaled)


def norm_back(grad_normed, normed, scaled):
    first_term = jnp.mean(grad_normed, axis=-1, keepdims=True)
    second_term = jnp.mean(grad_normed * normed, axis=-1, keepdims=True)
    return scaled * (grad_normed - first_term - normed * second_term)


def gelu_tanh(inputs):
    return jax.nn.gelu(inputs, approximate=True)


def rotary_tables(positions, head_size):
    halfway = head_size // 2
    inverse = 10000.0 ** (-2.0 * jnp.arange(halfway, dtype=jnp.float32) / head_size)
    angles = positions.astype(jnp.float32)[:, None] * inverse[None, :]
    return (jnp.cos(angles)[:, None, :], jnp.sin(angles)[:, None, :])


def rotate(inputs, cosine, sine_table):
    halfway = inputs.shape[-1] // 2
    first_half = inputs[..., :halfway]
    second_half = inputs[..., halfway:]
    return jnp.concatenate(
        [
            first_half * cosine - second_half * sine_table,
            second_half * cosine + first_half * sine_table,
        ],
        axis=-1,
    )


def rotate_back(grads, cosine, sine_table):
    halfway = grads.shape[-1] // 2
    first_half = grads[..., :halfway]
    second_half = grads[..., halfway:]
    return jnp.concatenate(
        [
            first_half * cosine + second_half * sine_table,
            second_half * cosine - first_half * sine_table,
        ],
        axis=-1,
    )


def segments(seq_lengths, row_count):
    seq_ends = jnp.cumsum(seq_lengths)
    seq_starts = seq_ends - seq_lengths
    row_index = jnp.arange(row_count, dtype=jnp.int32)
    segment = jnp.sum((row_index[:, None] >= seq_ends[None, :]).astype(jnp.int32), axis=1)
    onehot = segment[:, None] == jnp.arange(seq_lengths.shape[0], dtype=jnp.int32)[None, :]
    positions = row_index - jnp.sum(jnp.where(onehot, seq_starts[None, :], 0), axis=1)
    return (segment, onehot.astype(jnp.float32), positions)


def body(
    block_input,
    time_embed,
    seq_lengths,
    w_qkv,
    w_out,
    w_up,
    b_up,
    w_down,
    b_down,
    gain_one,
    gain_two,
    w_ada,
    b_ada,
    out_grad,
):
    own_width = block_input.shape[1]
    own_start = lax.axis_index("narrow") * own_width

    def own_cols(matrix):
        return lax.dynamic_slice_in_dim(matrix, own_start, own_width, 1)

    full_input, full_grad = (
        lax.all_gather(block_input, "narrow", axis=1, tiled=True),
        lax.all_gather(out_grad, "narrow", axis=1, tiled=True),
    )
    inputs = full_input.astype(jnp.float32)
    row_count = inputs.shape[0]
    model_width = inputs.shape[1]
    local_width = w_qkv.shape[2]
    local_heads = local_width // HD
    block_rows = min(512, row_count)
    block_count = row_count // block_rows
    segment, slot_table, positions = segments(seq_lengths[0], row_count)
    cosine, sine_table = rotary_tables(positions, HD)
    context, silu_back = jax.vjp(jax.nn.silu, time_embed)
    context_low = context.astype(jnp.bfloat16)
    modulation = jnp.dot(context_low, w_ada, preferred_element_type=jnp.float32) + b_ada
    pieces = [
        jnp.dot(
            slot_table,
            modulation[:, piece_index * model_width : (piece_index + 1) * model_width],
            precision=highest,
        )
        for piece_index in range(6)
    ]
    shift_one, scale_one, gate_one, shift_two, scale_two, gate_two = pieces
    normed_one, scaled_one = norm_stats(inputs)
    input_one = (normed_one * gain_one * (1.0 + scale_one) + shift_one).astype(jnp.bfloat16)
    projected = jnp.einsum("rd,tde->tre", input_one, w_qkv, preferred_element_type=jnp.float32)
    queries = (
        rotate(projected[0].reshape(row_count, local_heads, HD), cosine, sine_table) * 0.125
    ).astype(jnp.bfloat16)
    key_rows = rotate(projected[1].reshape(row_count, local_heads, HD), cosine, sine_table).astype(
        jnp.bfloat16
    )
    values = projected[2].reshape(row_count, local_heads, HD).astype(jnp.bfloat16)

    def attend(block_index):
        first_row = block_index * block_rows
        query_block = lax.dynamic_slice_in_dim(queries, first_row, block_rows, 0)
        segment_block = lax.dynamic_slice_in_dim(segment, first_row, block_rows, 0)
        scores = jnp.einsum(
            "qhd,khd->hqk", query_block, key_rows, preferred_element_type=jnp.float32
        )
        same_seq = segment_block[:, None] == segment[None, :]
        masked = jnp.where(same_seq[None], scores, -1e30)
        row_max = jnp.max(masked, axis=-1, keepdims=True)
        expos = jnp.exp(masked - row_max)
        row_total = jnp.sum(expos, axis=-1, keepdims=True)
        probabilities = (expos / row_total).astype(jnp.bfloat16)
        mixed_block = jnp.einsum(
            "hqk,khd->qhd", probabilities, values, preferred_element_type=jnp.float32
        ).astype(jnp.bfloat16)
        return (mixed_block, row_max[..., 0] + jnp.log(row_total[..., 0]))

    block_ids = jnp.arange(block_count, dtype=jnp.int32)
    mixed_blocks, log_totals = lax.map(attend, block_ids)
    mixed = mixed_blocks.reshape(row_count, local_width)
    attn_partial = jnp.dot(mixed, w_out, preferred_element_type=jnp.float32)
    attention = lax.psum(attn_partial.astype(jnp.bfloat16), "narrow").astype(jnp.float32)
    hidden_one = inputs + gate_one * attention
    normed_two, scaled_two = norm_stats(hidden_one)
    input_two = (normed_two * gain_two * (1.0 + scale_two) + shift_two).astype(jnp.bfloat16)
    pre_act = jnp.dot(input_two, w_up, preferred_element_type=jnp.float32) + b_up
    activated, gelu_back = jax.vjp(gelu_tanh, pre_act)
    act_low = activated.astype(jnp.bfloat16)
    feed_partial = jnp.dot(act_low, w_down, preferred_element_type=jnp.float32)
    feed_out = lax.psum(feed_partial.astype(jnp.bfloat16), "narrow").astype(jnp.float32) + b_down
    hidden_two = hidden_one + gate_two * feed_out
    block_output = own_cols(hidden_two).astype(jnp.bfloat16)
    grad_two = full_grad.astype(jnp.float32)
    grad_gate_two = grad_two * feed_out
    grad_feed = grad_two * gate_two
    grad_bias_down = jnp.sum(grad_feed, axis=0)
    feed_own_low = grad_feed.astype(jnp.bfloat16)
    grad_down = jnp.einsum("rf,rd->fd", act_low, feed_own_low, preferred_element_type=jnp.float32)
    grad_act = jnp.einsum("rd,fd->rf", feed_own_low, w_down, preferred_element_type=jnp.float32)
    grad_pre = gelu_back(grad_act)[0]
    grad_bias_up = jnp.sum(grad_pre, axis=0)
    pre_low = grad_pre.astype(jnp.bfloat16)
    grad_up = jnp.einsum("rd,rf->df", input_two, pre_low, preferred_element_type=jnp.float32)
    in_two_partial = jnp.einsum("rf,df->rd", pre_low, w_up, preferred_element_type=jnp.float32)
    grad_in_two = lax.psum(in_two_partial.astype(jnp.bfloat16), "narrow").astype(jnp.float32)
    grad_one = grad_two + norm_back(
        grad_in_two * (1.0 + scale_two) * gain_two, normed_two, scaled_two
    )
    grad_scale_two = grad_in_two * normed_two * gain_two
    grad_gain_two = jnp.sum(grad_in_two * normed_two * (1.0 + scale_two), axis=0)
    grad_gate_one = grad_one * attention
    attn_own_low = (grad_one * gate_one).astype(jnp.bfloat16)
    grad_out = jnp.einsum("rc,rd->cd", mixed, attn_own_low, preferred_element_type=jnp.float32)
    grad_mixed = (
        jnp.einsum("rd,cd->rc", attn_own_low, w_out, preferred_element_type=jnp.float32)
        .astype(jnp.bfloat16)
        .reshape(row_count, local_heads, HD)
    )

    def attend_back(totals, inputs_block):
        block_index, log_block = inputs_block
        grad_keys, grad_values = totals
        first_row = block_index * block_rows
        query_block = lax.dynamic_slice_in_dim(queries, first_row, block_rows, 0)
        segment_block = lax.dynamic_slice_in_dim(segment, first_row, block_rows, 0)
        upstream = lax.dynamic_slice_in_dim(grad_mixed, first_row, block_rows, 0)
        scores = jnp.einsum(
            "qhd,khd->hqk", query_block, key_rows, preferred_element_type=jnp.float32
        )
        same_seq = segment_block[:, None] == segment[None, :]
        probabilities = jnp.exp(jnp.where(same_seq[None], scores, -1e30) - log_block[:, :, None])
        grad_values = grad_values + jnp.einsum(
            "hqk,qhd->khd",
            probabilities.astype(jnp.bfloat16),
            upstream,
            preferred_element_type=jnp.float32,
        )
        grad_weights = jnp.einsum(
            "qhd,khd->hqk", upstream, values, preferred_element_type=jnp.float32
        )
        row_dot = jnp.sum(probabilities * grad_weights, axis=-1, keepdims=True)
        grad_scores = (probabilities * (grad_weights - row_dot)).astype(jnp.bfloat16)
        grad_query_block = jnp.einsum(
            "hqk,khd->qhd", grad_scores, key_rows, preferred_element_type=jnp.float32
        )
        grad_keys = grad_keys + jnp.einsum(
            "hqk,qhd->khd", grad_scores, query_block, preferred_element_type=jnp.float32
        )
        return ((grad_keys, grad_values), grad_query_block)

    empty = jnp.zeros((row_count, local_heads, HD), jnp.float32)
    (grad_keys, grad_values), grad_query_blocks = lax.scan(
        attend_back, (empty, empty), (block_ids, log_totals)
    )
    grad_query = rotate_back(
        grad_query_blocks.reshape(row_count, local_heads, HD) * 0.125, cosine, sine_table
    )
    grad_key = rotate_back(grad_keys, cosine, sine_table)
    grad_proj = jnp.stack(
        [
            grad_query.reshape(row_count, local_width),
            grad_key.reshape(row_count, local_width),
            grad_values.reshape(row_count, local_width),
        ]
    ).astype(jnp.bfloat16)
    grad_qkv = jnp.einsum("rd,tre->tde", input_one, grad_proj, preferred_element_type=jnp.float32)
    in_one_partial = jnp.einsum("tre,tde->rd", grad_proj, w_qkv, preferred_element_type=jnp.float32)
    grad_in_one = lax.psum(in_one_partial.astype(jnp.bfloat16), "narrow").astype(jnp.float32)
    full_input_grad = grad_one + norm_back(
        grad_in_one * (1.0 + scale_one) * gain_one, normed_one, scaled_one
    )
    input_grad = own_cols(full_input_grad)
    grad_scale_one = grad_in_one * normed_one * gain_one
    grad_gain_one = jnp.sum(grad_in_one * normed_one * (1.0 + scale_one), axis=0)
    row_grads = [
        grad_in_one,
        grad_scale_one,
        grad_gate_one,
        grad_in_two,
        grad_scale_two,
        grad_gate_two,
    ]
    grad_mod = jnp.concatenate(
        [
            jnp.einsum("rs,rd->sd", slot_table, piece_grad, precision=highest)
            for piece_grad in row_grads
        ],
        axis=1,
    )
    grad_bias_ada = jnp.sum(grad_mod, axis=0)
    mod_low = grad_mod.astype(jnp.bfloat16)
    grad_ada = jnp.einsum("sc,sm->cm", context_low, mod_low, preferred_element_type=jnp.float32)
    grad_context = jnp.einsum("sm,cm->sc", mod_low, w_ada, preferred_element_type=jnp.float32)
    time_grad = silu_back(grad_context)[0]
    (
        grad_qkv,
        grad_out,
        grad_up,
        grad_bias_up,
        grad_down,
        grad_bias_down,
        grad_gain_one,
        grad_gain_two,
        grad_ada,
        grad_bias_ada,
    ) = lax.psum(
        (
            grad_qkv,
            grad_out,
            grad_up,
            grad_bias_up,
            grad_down,
            grad_bias_down,
            grad_gain_one,
            grad_gain_two,
            grad_ada,
            grad_bias_ada,
        ),
        "wide",
    )
    return (
        block_output,
        input_grad,
        time_grad,
        grad_qkv,
        grad_out,
        grad_up,
        grad_bias_up,
        grad_down,
        grad_bias_down,
        grad_gain_one,
        grad_gain_two,
        grad_ada,
        grad_bias_ada,
    )


def solution(mesh):
    return jax.shard_map(
        body,
        mesh=mesh,
        in_specs=(
            P("wide", "narrow"),
            P("wide", None),
            P("wide", None),
            P(None, None, "narrow"),
            P("narrow", None),
            P(None, "narrow"),
            P("narrow"),
            P("narrow", None),
            P(),
            P(),
            P(),
            P(),
            P(),
            P("wide", "narrow"),
        ),
        out_specs=(
            P("wide", "narrow"),
            P("wide", "narrow"),
            P("wide", None),
            P(None, None, "narrow"),
            P("narrow", None),
            P(None, "narrow"),
            P("narrow"),
            P("narrow", None),
            P(),
            P(),
            P(),
            P(),
            P(),
        ),
        check_vma=False,
    )
```

profile of v0, /device:TPU:0, one launch (start us, length us, event | category | flops | bytes accessed | tf_op | source)
XLA Modules:
  0.0 797.1 jit_solution(9544113818319883742)
XLA Ops:
  16.2 46.6 %all-gather.3.cloned.1.call-done = bf16[1536,768]{0,1:T(8,128)(2,1)} async-done(((bf16[1536,192]{0,1:T(8,128)(2,1)}), bf16[1536,768]{0,1:T(8,128)(2,1)}) %all-gather.3.cloned.1.call-update) | async-done | bytes 2359312 | tf_op jit(solution)/shard_map/all_gather | solution.py:97
  67.4 5.5 add_convert_fusion.1
  75.3 30.8 %while.27 = (s32[]{:T(128)}, bf16[3,512,3,64]{1,3,2,0:T(8,128)(2,1)}, f32[3,3,512]{2,1,0:T(4,128)}, s32[3]{0:T(128)S(1)}, s32[1536]{0:T(1024)S(1)}, /*index=5*/b...) while((s32[]{:T(128)}, ...), condition=%wide.region_8.9_spmd, body=%wide.region_5.8_spmd.sunk | while | flops 626096640 | bytes 33093832 | solution.py:151
  112.6 4.8 fusion.81
  117.4 4.9 fusion.80
  122.3 83.8 %all-reduce.8.cloned.1.call-done = bf16[1536,768]{0,1:T(8,128)(2,1)} async-done(((bf16[1536,768]{0,1:T(8,128)(2,1)}), bf16[1536,768]{0,1:T(8,128)(2,1)}) %all-reduce.8.cloned.1.call-update) | async-done | bytes 2359312 | tf_op jit(solution)/shard_map/psum | solution.py:154
  206.1 7.1 fusion.122
  222.3 5.6 multiply_convert_fusion.2
  227.9 29.3 %all-gather.5.cloned.1.call-done = bf16[1536,768]{0,1:T(8,128)(2,1)} async-done(((bf16[1536,192]{0,1:T(8,128)(2,1)}), bf16[1536,768]{0,1:T(8,128)(2,1)}) %all-gather.5.cloned.1.call-update) | async-done | bytes 2359312 | tf_op jit(solution)/shard_map/all_gather | solution.py:98
  257.2 8.8 %fusion.124 = (f32[768]{0:T(1024)}, bf16[1536,768]{0,1:T(8,128)(2,1)S(1)}) fusion(f32[1536,768]{0,1:T(8,128)} %get-tuple-element.241, f32[768]{0:T(1024)S(1)} %copy-done.57, bf16[768,768]{1,0:T(8,128)(2,1)} %param.25, f32[1536,768]{0,1:T(8,128)} %fusion.81, bf16[1536,768]{0,1:T(8,128)(2,1)} %all-gather.5.cloned.1.call-done), kind=kOutput, calls=%fused_computation.190 | convolution fusion | flops 1841429760 | bytes 15341568 | tf_op jit(solution)/shard_map/rd,fd->rf/dot_general | solution.py:171
  271.0 5.4 convolution_convert_fusion.1
  276.4 89.1 %all-reduce.10.cloned.1.call-done = bf16[1536,768]{0,1:T(8,128)(2,1)} async-done(((bf16[1536,768]{0,1:T(8,128)(2,1)}), bf16[1536,768]{0,1:T(8,128)(2,1)}) %all-reduce.10.cloned.1.call-update) | async-done | bytes 2359312 | tf_op jit(solution)/shard_map/psum | solution.py:177
  365.5 6.4 multiply_reduce_fusion.1
  371.9 10.2 %multiply_convert_fusion.1 = (bf16[1536,768]{0,1:T(8,128)(2,1)S(1)}, f32[1536,768]{0,1:T(8,128)}, f32[768]{0:T(1024)}) fusion(f32[1536,768]{0,1:T(8,128)} %get-tuple-element.239, f32[1536]{0:T(1024)S(1)} %broadcast_multiply_fusion.2, f32[1536,768]{0,1:T(8,128)} %copy-done.2, f32[1536]{0:T(1024)S(1)} %broadcast_multiply_fusion.4, ...), kind=kLoop, calls=%fused_computation.77 | loop fusion | flops 18873600 | bytes 30701568 | tf_op jit(solution)/shard_map/convert_element_type | solution.py:184
  385.4 56.2 %while.28 = (s32[]{:T(128)}, f32[1536,3,64]{0,2,1:T(8,128)S(1)}, f32[1536,3,64]{0,2,1:T(8,128)S(1)}, f32[3,512,3,64]{1,3,2,0:T(8,128)}, s32[3]{0:T(128)}, /*inde...) while((s32[]{:T(128)}, f32[1536,3,64]{0,2,1:T(8,128)S(1)}, ...), condition=%wide.region_18.19_spmd.clone, body=%wide.region_16.18_spmd.clone.sunk | while | flops 1540225536 | bytes 84011280 | solution.py:224
  448.3 6.0 fusion.69
  454.4 5.9 fusion.113
  464.9 154.7 %all-reduce.14.cloned.1.call-done = (bf16[1536,768]{0,1:T(8,128)(2,1)}, bf16[1536,768]{0,1:T(8,128)(2,1)}) async-done(((bf16[1536,768]{0,1:T(8,128)(2,1)}, bf16[1536,768]{0,1:T(8,128)(2,1)}), (bf16[1536,768]{0,1:T(8,128)(2,1)}, bf16[1536,768]{0,1:T(8,128)(2,1)})) %all-reduce.14.cloned.1.call-update) | async-done | bytes 4718608 | tf_op jit(solution)/shard_map/psum | solution.py:162
  622.1 4.9 fusion.77
  627.1 5.0 fusion.76
  641.7 7.5 fusion.120
  649.2 28.1 %all-reduce = (f32[768]{0:T(1024)}, f32[768]{0:T(1024)}, f32[768]{0:T(1024)}, f32[768]{0:T(1024)}, f32[4608]{0:T(1024)}) all-reduce(f32[768]{0:T(1024)} %get-tuple-element.242, f32[768]{0:T(1024)} %get-tuple-element.224, f32[768]{0:T(1024)} %get-tuple-element.161, ...), channel_id=1, replica_groups=mesh['wide'=8,'narrow'=4] {'wide'}, use_global_device_ids=true, to_apply=%region_26.27 | all-reduce | flops 7680 | bytes 61440 | tf_op jit(solution)/shard_map/psum | solution.py:278
  682.7 4.8 dynamic-slice_add_fusion
  687.5 93.2 %all-reduce.12.cloned.1.call-done = (f32[3,768,192]{1,2,0:T(8,128)}, f32[192,768]{1,0:T(8,128)}, f32[768,768]{1,0:T(8,128)}, f32[768,768]{1,0:T(8,128)}, f32[128,4608]{1,0:T(8,128)}) async-done(((f32[3,768,192]{1,2,0:T(8,128)}, f32[192,768]{1,0:T(8,128)}, f32[768,768]{1,0:T(8,128)}, f32[768,768]{1,0:T(8,128)}, f32[128,4608]{1,0:T(8,128)}), (f32[3,768,192]{1,2,0:T(8,128)}, f32[192,768]{1,0:T(8,128)}, ...) | async-done | bytes 9437200 | tf_op jit(solution)/shard_map/psum | solution.py:278
  (253 shorter events, 159.7 us)
Async XLA Ops:
  7.2 215.2 %copy-start = (bf16[768,768]{1,0:T(8,128)(2,1)S(1)}, bf16[768,768]{1,0:T(8,128)(2,1)}, u32[]{:S(2)}) copy-start(bf16[768,768]{1,0:T(8,128)(2,1)} %param.23) | copy-start | bytes 3538948
  7.2 55.6 %all-gather.3.cloned.1.call-start = ((), (), s32[]{:S(2)}) async-start(), calls=%async_computation | async-start | bytes 2949120 | tf_op jit(solution)/shard_map/all_gather | solution.py:97
  7.9 198.2 %all-reduce.8.cloned.1.call-start = ((), (), s32[]{:S(2)}) async-start(), calls=%async_computation.1 | async-start | bytes 4718592 | tf_op jit(solution)/shard_map/psum | solution.py:154
  11.2 56.1 %copy-start.38 = (f32[3,4608]{1,0:T(4,128)}, f32[3,4608]{1,0:T(4,128)S(1)}, u32[]{:S(2)}) copy-start(f32[3,4608]{1,0:T(4,128)S(1)} %convolution_add_fusion) | copy-start | bytes 165892
  11.2 56.1 %copy-start.52 = (f32[768]{0:T(1024)S(1)}, f32[768]{0:T(1024)}, u32[]{:S(2)}) copy-start(f32[768]{0:T(1024)} %param.27) | copy-start | bytes 9220
  16.2 58.5 %copy-start.26 = (f32[1536,32]{0,1:T(8,128)}, f32[1536,32]{0,1:T(8,128)S(1)}, u32[]{:S(2)}) copy-start(f32[1536,32]{0,1:T(8,128)S(1)} %get-tuple-element.237) | copy-start | bytes 589828
  16.2 58.5 %copy-start.28 = (f32[1536,32]{0,1:T(8,128)}, f32[1536,32]{0,1:T(8,128)S(1)}, u32[]{:S(2)}) copy-start(f32[1536,32]{0,1:T(8,128)S(1)} %get-tuple-element.238) | copy-start | bytes 589828
  65.0 7.9 copy-start.42
  106.1 11.3 %copy-start.10 = (bf16[1536,3,64]{0,2,1:T(8,128)(2,1)}, bf16[1536,3,64]{0,2,1:T(8,128)(2,1)S(1)}, u32[]{:S(2)}) copy-start(bf16[1536,3,64]{0,2,1:T(8,128)(2,1)S(1)} %get-tuple-element.488) | copy-start | bytes 1769476
  108.1 9.3 %copy-start.17 = (bf16[24,8,3,512]{3,1,2,0:T(8,128)(2,1)}, bf16[24,8,3,512]{3,1,2,0:T(8,128)(2,1)S(1)}, u32[]{:S(2)}) copy-start(bf16[24,8,3,512]{3,1,2,0:T(8,128)(2,1)S(1)} %copy.77) | copy-start | bytes 1769476
  111.5 145.7 %all-gather.5.cloned.1.call-start = ((), (), s32[]{:S(2)}) async-start(), calls=%async_computation.2 | async-start | bytes 2949120 | tf_op jit(solution)/shard_map/all_gather | solution.py:98
  112.3 253.2 %all-reduce.10.cloned.1.call-start = ((), (), s32[]{:S(2)}) async-start(), calls=%async_computation.3 | async-start | bytes 4718592 | tf_op jit(solution)/shard_map/psum | solution.py:177
  213.2 7.7 copy-start.2
  270.9 348.6 %all-reduce.14.cloned.1.call-start = ((), (), s32[]{:S(2)}) async-start(), calls=%async_computation.5 | async-start | bytes 9437184 | tf_op jit(solution)/shard_map/psum | solution.py:162
  371.9 11.6 %copy-start.30 = (bf16[192,768]{1,0:T(8,128)(2,1)S(1)}, bf16[192,768]{1,0:T(8,128)(2,1)}, u32[]{:S(2)}) copy-start(bf16[192,768]{1,0:T(8,128)(2,1)} %param.22) | copy-start | bytes 884740
  448.0 332.7 %all-reduce.12.cloned.1.call-start = ((), (), s32[]{:S(2)}) async-start(), calls=%async_computation.4 | async-start | bytes 18874368 | tf_op jit(solution)/shard_map/psum | solution.py:278
  454.3 7.7 copy-start.25
  454.3 7.7 copy-start.33
  462.1 160.0 %copy-start.5 = (bf16[1536,768]{0,1:T(8,128)(2,1)S(1)}, bf16[1536,768]{0,1:T(8,128)(2,1)}, u32[]{:S(2)}) copy-start(bf16[1536,768]{0,1:T(8,128)(2,1)} %all-gather.3.cloned.1.call-done) | copy-start | bytes 7077892
  462.1 160.0 %copy-start.43 = (f32[1536]{0:T(1024)S(1)}, f32[1536]{0:T(1024)}, u32[]{:S(2)}) copy-start(f32[1536]{0:T(1024)} %copy-done.42) | copy-start | bytes 18436
  462.1 160.0 %copy-start.46 = (f32[1536]{0:T(1024)S(1)}, f32[1536]{0:T(1024)}, u32[]{:S(2)}) copy-start(f32[1536]{0:T(1024)} %copy-done.45) | copy-start | bytes 18436
  462.1 160.0 %copy-start.53 = (f32[768]{0:T(1024)S(1)}, f32[768]{0:T(1024)}, u32[]{:S(2)}) copy-start(f32[768]{0:T(1024)} %param.27) | copy-start | bytes 9220
  622.1 10.7 %slice-start = ((s8[4718592]{0:T(1024)(128)(4,1)}), s8[4194304]{0:T(1024)(128)(4,1)S(1)}, s32[]{:S(2)}) async-start(s8[4718592]{0:T(1024)(128)(4,1)} %bitcast.124), calls=%async_computation.6 | async-start | bytes 8388608
  641.7 37.0 %copy-start.19 = (bf16[128,4608]{1,0:T(8,128)(2,1)S(1)}, bf16[128,4608]{1,0:T(8,128)(2,1)}, u32[]{:S(2)}) copy-start(bf16[128,4608]{1,0:T(8,128)(2,1)} %param.29) | copy-start | bytes 3538948
  (46 other events, 191.4 us)
Sparse Core Ops, SparseCore 0:
  9.6 53.1 all-gather.2
  111.6 94.4 all-reduce.7
  207.7 49.5 all-gather.4
  271.0 94.4 all-reduce.9
  448.2 171.3 all-reduce.13
  641.1 139.5 all-reduce.11
where the time goes:
time: 804 us; the launch traced here: 797 us
  waiting for transfers between devices  498 us (62%)
  matrix products  158 us (20%)
  other arithmetic  63.7 us (8%)
  local copies, waits for them, and re-layouts  28.8 us (4%)
  blocking collectives  28.1 us (3%)
  between operations  15.3 us (2%)
    psum x1, waiting for transfers between devices, body(): lax.psum(feed_partial.astype(jnp.bfloat16), 'narrow').astype(jnp.float32)  155 us
    psum x1, waiting for transfers between devices, body(): lax.psum((grad_qkv, grad_out, grad_up, grad_bias_up, grad_down, grad_bias...  93.2 us
    psum x1, waiting for transfers between devices, body(): lax.psum(in_two_partial.astype(jnp.bfloat16), 'narrow').astype(jnp.float32)  89.1 us
    psum x1, waiting for transfers between devices, body(): lax.psum(attn_partial.astype(jnp.bfloat16), 'narrow').astype(jnp.float32)  83.8 us
    all_gather x1, waiting for transfers between devices, body(): lax.all_gather(block_input, 'narrow', axis=1, tiled=True)  46.6 us
    dot_general x6, matrix products, body(): jnp.dot(slot_table, modulation[:, piece_index * model_width:(piece_index...  30.2 us
    all_gather x1, waiting for transfers between devices, body(): lax.all_gather(out_grad, 'narrow', axis=1, tiled=True)  29.3 us
    psum x1, blocking collectives, body(): lax.psum((grad_qkv, grad_out, grad_up, grad_bias_up, grad_down, grad_bias...  28.1 us
  transfers between devices with their start and end apart: 6, of which 6 were waited for; matrix products, arithmetic and copies ran while one was open for 9% of the time, Pallas kernels for 0%

commit v1 on v0

v1 whole, which is shorter than its diff:
```python
import functools

import jax
import jax.numpy as jnp
from jax import lax
from jax.experimental import pallas as pl
from jax.experimental.pallas import tpu as pltpu
from jax.sharding import PartitionSpec as P

HD = 64
epsilon = 1e-05
highest = lax.Precision.HIGHEST
MESH = pl.DeviceIdType.MESH
CHUNKS = 3
F32 = jnp.float32
BF16 = jnp.bfloat16


def place():
    w = lax.axis_index("wide")
    z = lax.axis_index("narrow")
    return w, z, w % 2, (w // 2) % 2, (w // 4) % 2


def flip(w, bit, step):
    return w + step * (1 - 2 * bit)


def remote(src, dst, send, recv, device):
    return pltpu.make_async_remote_copy(
        src_ref=src, dst_ref=dst, send_sem=send, recv_sem=recv, device_id=device, device_id_type=MESH
    )


def greet(devices):
    barrier = pltpu.get_barrier_semaphore()
    for device in devices:
        pl.semaphore_signal(barrier, inc=1, device_id=device, device_id_type=MESH)
    pl.semaphore_wait(barrier, len(devices))


def column_peers(w, z, c):
    return [
        (w if same else flip(w, c, 1), (z + dz) % 4) for same in (1, 0) for dz in range(4) if not (same and dz == 0)
    ]


def gather_kernel(
    x, dy, w_attn, w_up, w_down, b_up, info,
    x_out, dy_out, w_out, b_out, info_out,
    x_send, x_recv, pair_send, pair_recv, local_sem, home_send, block_recv, ring_send, plane_send, b_send, b_recv,
):
    w, z, c, bx, by = place()
    part = x.shape[0] // 4
    rows = w_attn.shape[0] // 4
    across_x, across_y = flip(w, bx, 2), flip(w, by, 4)
    other = flip(w, c, 1)
    greet(column_peers(w, z, c) + [(across_x, z), (across_y, z)])
    block_a = pl.ds(pl.multiple_of(bx * rows, rows), rows)
    block_b = pl.ds(pl.multiple_of((2 + by) * rows, rows), rows)

    info_copy = remote(info, info_out, pair_send.at[2], pair_recv.at[2], (other, z))
    info_copy.start()

    def exchange(k, source, target):
        for j in range(4):
            device = (w - c + j % 2, 2 * c + j // 2)
            mine = (c == j % 2) & (device[1] == z)
            block = source.at[pl.ds(j * part, part)]

            @pl.when(mine)
            def _():
                pltpu.make_async_copy(block, target.at[j % 2, z], x_recv.at[k, z]).start()

            @pl.when(jnp.logical_not(mine))
            def _():
                remote(block, target.at[j % 2, z], x_send.at[k, j], x_recv.at[k, z], device).start()

    def exchange_sent(k, source, target):
        for j in range(4):
            mine = (c == j % 2) & (2 * c + j // 2 == z)

            @pl.when(jnp.logical_not(mine))
            def _():
                block = source.at[pl.ds(j * part, part)]
                remote(block, target.at[j % 2, z], x_send.at[k, j], x_recv.at[k, z], (w, z)).wait_send()

    def exchange_done(k, source, target):
        for slot in range(4):
            pltpu.make_async_copy(source.at[pl.ds(0, part)], target.at[c, slot], x_recv.at[k, slot]).wait()
        pair = remote(target.at[c], target.at[c], pair_send.at[k], pair_recv.at[k], (other, z))
        pair.start()

    def pair_done(k, target):
        remote(target.at[c], target.at[1 - c], pair_send.at[k], pair_recv.at[k], (other, z)).wait_recv()

    exchange(0, x, x_out)
    for dz in range(1, 4):
        remote(b_up, b_out.at[z], b_send.at[dz], b_recv.at[dz], (w, (z + dz) % 4)).start()
    pltpu.make_async_copy(b_up, b_out.at[z], b_send.at[0]).start()

    chunks = (w_attn, w_up, w_down)
    far = [(z - 2 * c - q) % 4 for q in range(2)]
    for t in range(CHUNKS):
        for q in range(2):

            @pl.when(far[q] == 0)
            def _():
                pltpu.make_async_copy(chunks[t], w_out.at[t, q], local_sem.at[t]).start()
                for n, block in enumerate((block_a, block_b)):
                    for m, step in enumerate((1, 3)):
                        remote(
                            chunks[t].at[block], w_out.at[t, q, block], home_send.at[t, 2 * n + m],
                            block_recv.at[t, q, n], (w, (z + step) % 4),
                        ).start()

    exchange(1, dy, dy_out)
    exchange_done(0, x, x_out)

    def landed(t, q, n, block):
        pltpu.make_async_copy(w_out.at[t, q, block], w_out.at[t, q, block], block_recv.at[t, q, n]).wait()

    def ring(t, q, n, block, step):
        return remote(
            w_out.at[t, q, block], w_out.at[t, q, block], ring_send.at[t, q], block_recv.at[t, q, n],
            (w, (z + step) % 4),
        )

    def plane(t, q, n, block):
        return remote(
            w_out.at[t, q, block], w_out.at[t, q, block], plane_send.at[t, q, n], block_recv.at[t, q, 2 + n],
            ((across_x, across_y)[n], z),
        )

    for t in range(CHUNKS):
        for q in range(2):

            @pl.when(far[q] == 1)
            def _():
                landed(t, q, 0, block_a)
                ring(t, q, 0, block_a, 1).start()
                plane(t, q, 0, block_a).start()
                landed(t, q, 1, block_b)
                plane(t, q, 1, block_b).start()

            @pl.when(far[q] == 3)
            def _():
                landed(t, q, 1, block_b)
                ring(t, q, 1, block_b, 3).start()
                plane(t, q, 1, block_b).start()
                landed(t, q, 0, block_a)
                plane(t, q, 0, block_a).start()

        for q in range(2):

            @pl.when(far[q] == 2)
            def _():
                landed(t, q, 0, block_a)
                plane(t, q, 0, block_a).start()
                landed(t, q, 1, block_b)
                plane(t, q, 1, block_b).start()

    exchange_done(1, dy, dy_out)
    other_a = pl.ds(pl.multiple_of((1 - bx) * rows, rows), rows)
    other_b = pl.ds(pl.multiple_of((3 - by) * rows, rows), rows)
    for t in range(CHUNKS):
        for q in range(2):

            @pl.when(far[q] == 0)
            def _():
                pltpu.make_async_copy(chunks[t], w_out.at[t, q], local_sem.at[t]).wait()
                for n, block in enumerate((block_a, block_b)):
                    for m, step in enumerate((1, 3)):
                        remote(
                            chunks[t].at[block], w_out.at[t, q, block], home_send.at[t, 2 * n + m],
                            block_recv.at[t, q, n], (w, (z + step) % 4),
                        ).wait_send()

            @pl.when(far[q] == 1)
            def _():
                ring(t, q, 0, block_a, 1).wait_send()

            @pl.when(far[q] == 3)
            def _():
                ring(t, q, 1, block_b, 3).wait_send()

            @pl.when(far[q] != 0)
            def _():
                plane(t, q, 0, block_a).wait_send()
                plane(t, q, 1, block_b).wait_send()
                landed(t, q, 2, other_a)
                landed(t, q, 3, other_b)

    pair_done(0, x_out)
    pair_done(1, dy_out)
    for k, (source, target) in enumerate(((x, x_out), (dy, dy_out))):
        exchange_sent(k, source, target)
        remote(target.at[c], target.at[c], pair_send.at[k], pair_recv.at[k], (other, z)).wait_send()
    info_copy.wait()
    for dz in range(1, 4):
        remote(b_up, b_out.at[(z - dz) % 4], b_send.at[dz], b_recv.at[dz], (w, (z + dz) % 4)).wait()
    pltpu.make_async_copy(b_up, b_out.at[z], b_send.at[0]).wait()


def gather_all(x, dy, w_attn, w_up, w_down, b_up, info):
    rows, width = x.shape
    size = w_attn.shape[0]
    any_space = pl.BlockSpec(memory_space=pl.ANY)
    dma = pltpu.SemaphoreType.DMA
    return pl.pallas_call(
        gather_kernel,
        out_shape=(
            jax.ShapeDtypeStruct((2, 4, rows // 4, width), BF16),
            jax.ShapeDtypeStruct((2, 4, rows // 4, width), BF16),
            jax.ShapeDtypeStruct((CHUNKS, 2, size, size), BF16),
            jax.ShapeDtypeStruct((4,) + b_up.shape, F32),
            jax.ShapeDtypeStruct(info.shape, F32),
        ),
        in_specs=[any_space] * 7,
        out_specs=(any_space,) * 5,
        scratch_shapes=[
            dma((2, 4)), dma((2, 4)), dma((3,)), dma((3,)), dma((CHUNKS,)), dma((CHUNKS, 4)), dma((CHUNKS, 2, 4)),
            dma((CHUNKS, 2)), dma((CHUNKS, 2, 2)), dma((4,)), dma((4,)),
        ],
        compiler_params=pltpu.CompilerParams(collective_id=0, has_side_effects=True),
        name="gather_all",
    )(x, dy, w_attn, w_up, w_down, b_up, info)


def reduce_kernel(
    n_wide, sub, grads, out_rows, in_rows,
    g_out, out_o, in_o,
    near, ring_in, own, mids, finals,
    o_send, o_recv, near_send, near_recv, ring_send, ring_recv, mid_send, mid_recv, push_send, push_recv, pair_send,
    pair_recv,
):
    w, z, c, bx, by = place()
    members = n_wide // 4
    plane_count = n_wide // 2
    rows = grads.shape[2] // 4
    plane_at = w // 2
    across = (flip(w, bx, 2), flip(w, by, 4))
    other = flip(w, c, 1)
    plane_peers = [((w + step) % n_wide, z) for step in range(1, n_wide)]
    z_peers = [(w, (z + dz) % 4) for dz in range(1, 4)]
    greet(plane_peers + z_peers + [(other, (z + dz) % 4) for dz in range(1, 4)])
    blocks = (
        pl.ds(pl.multiple_of(bx * rows, rows), rows),
        pl.ds(pl.multiple_of((2 + by) * rows, rows), rows),
    )
    others = (
        pl.ds(pl.multiple_of((1 - bx) * rows, rows), rows),
        pl.ds(pl.multiple_of((3 - by) * rows, rows), rows),
    )
    far = [(z - 2 * c - q) % 4 for q in range(2)]
    home = c == z // 2
    member = (w // 4, bx + 2 * (w // 8))
    part = out_rows.shape[1] // 2

    def near_copy(t, q, n):
        return remote(
            grads.at[t, q, others[n]], near.at[t, q, n], near_send.at[t, q, n], near_recv.at[t, q, n], (across[n], z)
        )

    order = (2, 1, 0)
    for t in order:
        for q in range(2):
            for n in range(2):
                near_copy(t, q, n).start()

    def spread(k, source, target, start):
        for dest in range(4):
            device = (w - c + z // 2, dest)
            mine = (c == z // 2) & (z == dest)
            slot = 2 * (z % 2) + c
            block = source.at[dest, pl.ds(pl.multiple_of(c * part, part), part)]

            @pl.when(mine)
            def _():
                if start:
                    pltpu.make_async_copy(block, target.at[slot], o_recv.at[k, slot]).start()

            @pl.when(jnp.logical_not(mine))
            def _():
                copy = remote(block, target.at[slot], o_send.at[k, dest], o_recv.at[k, slot], device)
                copy.start() if start else copy.wait_send()

    spread(0, out_rows, out_o, True)
    spread(1, in_rows, in_o, True)

    def tiles(step):
        def run(i, carry):
            step(pl.ds(pl.multiple_of(i * 16, 16), 16))
            return carry

        lax.fori_loop(0, rows // 16, run, 0)

    def ring_copy(t, q, n, slot, step):
        return remote(
            own.at[t, q, n, pl.ds(0, rows)], ring_in.at[t, q, slot], ring_send.at[t, q, n], ring_recv.at[t, q, slot],
            (w, (z + step) % 4),
        )

    def near_add(t, q, n):
        near_copy(t, q, n).wait_recv()
        base = (bx, 2 + by)[n] * rows

        def step(s):
            place_rows = pl.ds(pl.multiple_of(base + s.start, 16), 16)
            own[t, q, n, s] = (grads[t, q, place_rows].astype(F32) + near[t, q, n, s].astype(F32)).astype(BF16)

        tiles(step)

    def arrived(t, q, slot):
        pltpu.make_async_copy(ring_in.at[t, q, slot], ring_in.at[t, q, slot], ring_recv.at[t, q, slot]).wait()

    def add_in(t, q, n, slots):
        def step(s):
            total = own[t, q, n, s].astype(F32)
            for slot in slots:
                total = total + ring_in[t, q, slot, s].astype(F32)
            own[t, q, n, s] = total.astype(BF16)

        tiles(step)

    def mid_copy(t, n, m):
        device_w = ((2 * m + bx) * 2 + c, (4 * (m // 2) + 2 * by + m % 2) * 2 + c)[n]
        return remote(
            own.at[t, z % 2, n, pl.ds(m * sub, sub)], mids.at[t, n, member[n]], mid_send.at[t, n, m],
            mid_recv.at[t, n, member[n]], (device_w, z),
        )

    def push_copy(t, n, step):
        target = g_out.at[t, (bx, 2 + by)[n], pl.ds(pl.multiple_of(member[n] * sub, sub), sub)]
        return remote(
            finals.at[t, n], target, push_send.at[t, n, step], push_recv.at[t, n, step],
            ((w + 2 * step) % n_wide, z),
        )

    def local_copy(t, n):
        target = g_out.at[t, (bx, 2 + by)[n], pl.ds(pl.multiple_of(member[n] * sub, sub), sub)]
        return pltpu.make_async_copy(finals.at[t, n], target, push_recv.at[t, n, 0])

    def pair_copy(t):
        return remote(g_out.at[t], g_out.at[t], pair_send.at[t], pair_recv.at[t], (other, z))

    for t in order:
        for q in range(2):
            for n in range(2):
                near_add(t, q, n)

            @pl.when(far[q] == 2)
            def _():
                ring_copy(t, q, 0, 0, 3).start()
                ring_copy(t, q, 1, 0, 1).start()

            @pl.when(far[q] == 1)
            def _():
                ring_copy(t, q, 1, 1, 3).start()

            @pl.when(far[q] == 3)
            def _():
                ring_copy(t, q, 0, 2, 1).start()

    for t in order:
        for q in range(2):

            @pl.when(far[q] == 1)
            def _():
                arrived(t, q, 0)
                add_in(t, q, 0, (0,))
                ring_copy(t, q, 0, 0, 3).start()

            @pl.when(far[q] == 3)
            def _():
                arrived(t, q, 0)
                add_in(t, q, 1, (0,))
                ring_copy(t, q, 1, 3, 1).start()

    for t in order:
        for q in range(2):

            @pl.when(far[q] == 0)
            def _():
                for slot in range(4):
                    arrived(t, q, slot)
                add_in(t, q, 0, (0, 2))
                add_in(t, q, 1, (1, 3))
                for n in range(2):
                    for m in range(members):

                        @pl.when(member[n] != m)
                        def _():
                            mid_copy(t, n, m).start()

    for t in order:

        @pl.when(home)
        def _():
            for n in range(2):
                for m in range(members):

                    @pl.when(member[n] != m)
                    def _():
                        pltpu.make_async_copy(mids.at[t, n, m], mids.at[t, n, m], mid_recv.at[t, n, m]).wait()

                first = member[n] * sub

                def run(i, carry):
                    s = pl.ds(pl.multiple_of(i * 16, 16), 16)
                    total = own[t, z % 2, n, pl.ds(pl.multiple_of(first + i * 16, 16), 16)].astype(F32)
                    for m in range(members):
                        term = mids[t, n, m, s].astype(F32)
                        total = total + jnp.where(member[n] == m, 0.0, term)
                    finals[t, n, s] = total.astype(BF16)
                    return carry

                lax.fori_loop(0, sub // 16, run, 0)
                local_copy(t, n).start()
                for step in range(1, plane_count):
                    push_copy(t, n, step).start()

    for t in order:

        @pl.when(home)
        def _():
            for n in range(2):
                local_copy(t, n).wait()
                for step in range(1, plane_count):
                    push_copy(t, n, step).wait_recv()
            pair_copy(t).start()

    for t in order:

        @pl.when(home)
        def _():
            pair_copy(t).wait_send()
            for n in range(2):
                for step in range(1, plane_count):
                    push_copy(t, n, step).wait_send()
                for m in range(members):

                    @pl.when(member[n] != m)
                    def _():
                        mid_copy(t, n, m).wait_send()

        @pl.when(jnp.logical_not(home))
        def _():
            pair_copy(t).wait_recv()

        for q in range(2):
            for n in range(2):
                near_copy(t, q, n).wait_send()

            @pl.when(far[q] != 0)
            def _():
                for n in range(2):
                    ring_copy(t, q, n, 0, 1).wait_send()

    for k, (source, target) in enumerate(((out_rows, out_o), (in_rows, in_o))):
        for slot in range(4):
            pltpu.make_async_copy(source.at[0, pl.ds(0, part)], target.at[slot], o_recv.at[k, slot]).wait()
        spread(k, source, target, False)


def reduce_all(n_wide, grads, out_rows, in_rows):
    size = grads.shape[-1]
    rows = size // 4
    members = n_wide // 4
    sub = -(-rows // members // 16) * 16
    part, width = out_rows.shape[1] // 2, out_rows.shape[2]
    any_space = pl.BlockSpec(memory_space=pl.ANY)
    dma = pltpu.SemaphoreType.DMA
    spread = max(rows, members * sub)
    g_out, out_o, in_o = pl.pallas_call(
        functools.partial(reduce_kernel, n_wide, sub),
        out_shape=(
            jax.ShapeDtypeStruct((CHUNKS, 4, members * sub, size), BF16),
            jax.ShapeDtypeStruct((4, part, width), BF16),
            jax.ShapeDtypeStruct((4, part, width), BF16),
        ),
        in_specs=[pl.BlockSpec(memory_space=pltpu.VMEM), any_space, any_space],
        out_specs=(any_space,) * 3,
        scratch_shapes=[
            pltpu.VMEM((CHUNKS, 2, 2, rows, size), BF16),
            pltpu.VMEM((CHUNKS, 2, 4, rows, size), BF16),
            pltpu.VMEM((CHUNKS, 2, 2, spread, size), BF16),
            pltpu.VMEM((CHUNKS, 2, members, sub, size), BF16),
            pltpu.VMEM((CHUNKS, 2, sub, size), BF16),
            dma((2, 4)), dma((2, 4)), dma((CHUNKS, 2, 2)), dma((CHUNKS, 2, 2)), dma((CHUNKS, 2, 2)), dma((CHUNKS, 2, 4)),
            dma((CHUNKS, 2, members)), dma((CHUNKS, 2, members)), dma((CHUNKS, 2, n_wide // 2)),
            dma((CHUNKS, 2, n_wide // 2)), dma((CHUNKS,)), dma((CHUNKS,)),
        ],
        compiler_params=pltpu.CompilerParams(
            collective_id=1, has_side_effects=True, vmem_limit_bytes=56 * 1024 * 1024
        ),
        name="reduce_all",
    )(grads, out_rows, in_rows)
    return g_out[:, :, :rows].reshape(CHUNKS, size, size), out_o, in_o


def norm_stats(inputs):
    row_mean = jnp.mean(inputs, axis=-1, keepdims=True)
    centered = inputs - row_mean
    variance = jnp.mean(centered * centered, axis=-1, keepdims=True)
    scaled = lax.rsqrt(variance + epsilon)
    return (centered * scaled, scaled)


def norm_back(grad_normed, normed, scaled):
    first_term = jnp.mean(grad_normed, axis=-1, keepdims=True)
    second_term = jnp.mean(grad_normed * normed, axis=-1, keepdims=True)
    return scaled * (grad_normed - first_term - normed * second_term)


def gelu_tanh(inputs):
    return jax.nn.gelu(inputs, approximate=True)


def rotary_tables(positions, head_size):
    halfway = head_size // 2
    inverse = 10000.0 ** (-2.0 * jnp.arange(halfway, dtype=F32) / head_size)
    angles = positions.astype(F32)[:, None] * inverse[None, :]
    return (jnp.cos(angles)[:, None, :], jnp.sin(angles)[:, None, :])


def rotate(inputs, cosine, sine_table):
    halfway = inputs.shape[-1] // 2
    first_half = inputs[..., :halfway]
    second_half = inputs[..., halfway:]
    return jnp.concatenate(
        [
            first_half * cosine - second_half * sine_table,
            second_half * cosine + first_half * sine_table,
        ],
        axis=-1,
    )


def body(
    n_wide,
    block_input,
    time_embed,
    seq_lengths,
    w_qkv,
    w_out,
    w_up,
    b_up,
    w_down,
    b_down,
    gain_one,
    gain_two,
    w_ada,
    b_ada,
    out_grad,
):
    w, z, core, _, _ = place()
    row_count, own_width = block_input.shape
    half = row_count // 2
    size = w_qkv.shape[1]
    slots, cond = time_embed.shape
    quarter = w_qkv.shape[2]
    heads = 2 * quarter // HD
    pair_index = [(i, i ^ 1) for i in range(n_wide)]

    def long_start(lengths):
        slot = jnp.argmax(lengths)
        return slot, jnp.sum(jnp.where(jnp.arange(slots) < slot, lengths, 0))

    lengths = seq_lengths[0]
    own_slot, own_start = long_start(lengths)

    def turn(rows, shift):
        return lax.dynamic_slice_in_dim(jnp.concatenate([rows, rows], axis=0), shift, row_count, 0)

    info = jnp.concatenate(
        [time_embed, jnp.pad(lengths.astype(F32)[None], ((0, 0), (0, cond - slots))), jnp.zeros((8 - slots - 1, cond))]
    )
    w_attn = jnp.concatenate([jnp.swapaxes(w_qkv, 1, 2).reshape(-1, size), w_out], axis=0)
    b_rows = jnp.pad(b_up.reshape(-1, 128), ((0, 2), (0, 0)))
    x_parts, dy_parts, weights, b_parts, info_other = gather_all(
        turn(block_input, own_start), turn(out_grad, own_start), w_attn, w_up, w_down, b_rows, info
    )

    def whole(parts):
        return jnp.swapaxes(parts, 1, 2).reshape(half, size)

    inputs = whole(x_parts).astype(F32)
    grad_two = whole(dy_parts).astype(F32)
    info = jnp.where(core == z // 2, info, info_other)
    times = info[:slots]
    lengths = info[slots, :slots].astype(jnp.int32)
    long_slot, _ = long_start(lengths)
    second_half = z % 2 == 1
    slot_a = jnp.where(second_half, (long_slot + 1) % slots, long_slot)
    slot_b = jnp.where(second_half, (long_slot + 2) % slots, long_slot)
    bound = jnp.where(second_half, lengths[slot_a], half)
    row_ids = jnp.arange(half, dtype=jnp.int32)
    first = row_ids < bound
    positions = jnp.where(first, row_ids, row_ids - bound)
    cosine, sine_table = rotary_tables(positions, HD)
    context = jax.nn.silu(times)
    context_low = context.astype(BF16)
    modulation = jnp.dot(context_low, w_ada, preferred_element_type=F32) + b_ada
    mod_a, mod_b = modulation[slot_a], modulation[slot_b]
    pieces = [
        jnp.where(first[:, None], mod_a[None, i * size : (i + 1) * size], mod_b[None, i * size : (i + 1) * size])
        for i in range(6)
    ]
    shift_one, scale_one, gate_one, shift_two, scale_two, gate_two = pieces
    w_qkv_t = weights[0, :, : 3 * quarter].reshape(2, 3, quarter, size)
    w_out_own = weights[0, :, 3 * quarter :].reshape(2 * quarter, size)
    w_up_own, w_down_own = weights[1], weights[2].reshape(-1, size)
    b_own = lax.dynamic_slice_in_dim(b_parts, 2 * core, 2, 0)[:, :6].reshape(-1)

    normed_one, scaled_one = norm_stats(inputs)
    input_one = (normed_one * gain_one * (1.0 + scale_one) + shift_one).astype(BF16)
    projected = jnp.einsum("rd,qted->trqe", input_one, w_qkv_t, preferred_element_type=F32)
    projected = projected.reshape(3, half, heads, HD)
    queries = (rotate(projected[0], cosine, sine_table) * 0.125).astype(BF16)
    key_rows = rotate(projected[1], cosine, sine_table).astype(BF16)
    values = projected[2].astype(BF16)
    same_seq = first[:, None] == first[None, :]
    scores = jnp.einsum("qhd,khd->hqk", queries, key_rows, preferred_element_type=F32)
    masked = jnp.where(same_seq[None], scores, -1e30)
    row_max = jnp.max(masked, axis=-1, keepdims=True)
    expos = jnp.exp(masked - row_max)
    row_total = jnp.sum(expos, axis=-1, keepdims=True)
    probabilities = expos / row_total
    low_probs = probabilities.astype(BF16)
    mixed = jnp.einsum("hqk,khd->qhd", low_probs, values, preferred_element_type=F32)
    mixed = mixed.astype(BF16).reshape(half, heads * HD)

    def both_cores(partial):
        partial = partial.astype(BF16)
        return partial.astype(F32) + lax.ppermute(partial, "wide", pair_index).astype(F32)

    attention = both_cores(jnp.dot(mixed, w_out_own, preferred_element_type=F32))
    hidden_one = inputs + gate_one * attention
    normed_two, scaled_two = norm_stats(hidden_one)
    input_two = (normed_two * gain_two * (1.0 + scale_two) + shift_two).astype(BF16)
    pre_act = jnp.einsum("rd,qdf->rqf", input_two, w_up_own, preferred_element_type=F32).reshape(half, -1) + b_own
    activated, gelu_back = jax.vjp(gelu_tanh, pre_act)
    act_low = activated.astype(BF16)
    feed_out = both_cores(jnp.dot(act_low, w_down_own, preferred_element_type=F32)) + b_down
    hidden_two = hidden_one + gate_two * feed_out
    block_output = hidden_two.astype(BF16)

    grad_gate_two = grad_two * feed_out
    grad_feed = grad_two * gate_two
    grad_bias_down = jnp.sum(grad_feed, axis=0)
    feed_low = grad_feed.astype(BF16)
    grad_down = jnp.einsum("rf,rd->fd", act_low, feed_low, preferred_element_type=F32)
    grad_act = jnp.einsum("rd,fd->rf", feed_low, w_down_own, preferred_element_type=F32)
    grad_pre = gelu_back(grad_act)[0]
    grad_bias_up = jnp.sum(grad_pre, axis=0)
    pre_low = grad_pre.astype(BF16).reshape(half, 2, -1)
    grad_up = jnp.einsum("rd,rqf->qdf", input_two, pre_low, preferred_element_type=F32)
    grad_in_two = both_cores(jnp.einsum("rqf,qdf->rd", pre_low, w_up_own, preferred_element_type=F32))
    grad_one = grad_two + norm_back(grad_in_two * (1.0 + scale_two) * gain_two, normed_two, scaled_two)
    grad_scale_two = grad_in_two * normed_two * gain_two
    grad_gain_two = jnp.sum(grad_in_two * normed_two * (1.0 + scale_two), axis=0)
    grad_gate_one = grad_one * attention
    attn_low = (grad_one * gate_one).astype(BF16)
    grad_out = jnp.einsum("rc,rd->cd", mixed, attn_low, preferred_element_type=F32)
    grad_mixed = jnp.einsum("rd,cd->rc", attn_low, w_out_own, preferred_element_type=F32)
    grad_mixed = grad_mixed.astype(BF16).reshape(half, heads, HD)
    grad_values = jnp.einsum("hqk,qhd->khd", low_probs, grad_mixed, preferred_element_type=F32)
    grad_weights = jnp.einsum("qhd,khd->hqk", grad_mixed, values, preferred_element_type=F32)
    row_dot = jnp.sum(probabilities * grad_weights, axis=-1, keepdims=True)
    grad_scores = (probabilities * (grad_weights - row_dot)).astype(BF16)
    grad_query = jnp.einsum("hqk,khd->qhd", grad_scores, key_rows, preferred_element_type=F32)
    grad_key = jnp.einsum("hqk,qhd->khd", grad_scores, queries, preferred_element_type=F32)
    grad_query = rotate(grad_query * 0.125, cosine, -sine_table)
    grad_key = rotate(grad_key, cosine, -sine_table)
    grad_proj = jnp.stack([grad_query, grad_key, grad_values]).astype(BF16).reshape(3, half, 2, quarter)
    grad_qkv = jnp.einsum("trqe,rd->qted", grad_proj, input_one, preferred_element_type=F32)
    grad_in_one = both_cores(jnp.einsum("trqe,qted->rd", grad_proj, w_qkv_t, preferred_element_type=F32))
    input_grad = grad_one + norm_back(grad_in_one * (1.0 + scale_one) * gain_one, normed_one, scaled_one)
    grad_scale_one = grad_in_one * normed_one * gain_one
    grad_gain_one = jnp.sum(grad_in_one * normed_one * (1.0 + scale_one), axis=0)
    row_grads = [grad_in_one, grad_scale_one, grad_gate_one, grad_in_two, grad_scale_two, grad_gate_two]
    slot_table = jnp.stack([first, jnp.logical_not(first)], axis=1).astype(F32)
    grad_mod = jnp.concatenate(
        [jnp.einsum("rs,rd->sd", slot_table, piece_grad, precision=highest) for piece_grad in row_grads], axis=1
    )

    shared = jnp.concatenate([grad_mod.reshape(-1), grad_bias_down, grad_gain_one, grad_gain_two])
    share = shared.shape[0] // 2
    message = jnp.concatenate([lax.dynamic_slice_in_dim(shared, core * share, share, 0), grad_bias_up]).astype(BF16)
    gathered = lax.all_gather(message, ("wide", "narrow"))
    gathered = gathered.reshape(n_wide // 2, 2, 4, -1)

    grads = jnp.stack(
        [
            jnp.concatenate([grad_qkv.reshape(2, 3 * quarter, size), grad_out.reshape(2, quarter, size)], axis=1),
            grad_up,
            grad_down.reshape(2, size, size),
        ]
    ).astype(BF16)

    def split(rows):
        return jnp.swapaxes(rows.astype(BF16).reshape(half, 4, own_width), 0, 1)

    g_own, out_parts, in_parts = reduce_all(n_wide, grads, split(block_output), split(input_grad))

    def unturn(parts):
        return turn(parts.reshape(row_count, own_width), (row_count - own_start) % row_count)

    final_output = unturn(out_parts)
    final_input_grad = unturn(in_parts).astype(F32)

    all_shared = jnp.swapaxes(gathered[..., :share], 1, 2).reshape(n_wide // 2, 4, 2 * share)
    all_mod = all_shared[..., : 12 * size].reshape(n_wide // 2, 4, 2, 6 * size)
    sums = jnp.sum(all_shared[..., 12 * size :].astype(F32), axis=(0, 1)).reshape(3, size)
    grad_bias_down, grad_gain_one, grad_gain_two = sums[0], sums[1], sums[2]
    up_parts = lax.dynamic_index_in_dim(gathered[..., share:], z // 2, 1, False)
    up_sum = jnp.sum(up_parts.astype(F32), axis=(0, 1)).reshape(2, size)
    grad_bias_up = lax.dynamic_index_in_dim(up_sum, z % 2, 0, False)

    all_mod = all_mod.reshape(n_wide, 2, 2, 6 * size)
    all_info = lax.all_gather(
        jnp.concatenate([time_embed, jnp.pad(seq_lengths.astype(F32), ((0, 0), (0, cond - slots)))]), "wide"
    )
    all_lengths = all_info[:, slots, :slots].astype(jnp.int32)
    long_slots = jnp.argmax(all_lengths, axis=1)
    all_context = jax.nn.silu(all_info[:, :slots]).astype(BF16)
    row_slots = jnp.stack(
        [long_slots, long_slots, (long_slots + 1) % slots, (long_slots + 2) % slots], axis=1
    )
    rows_context = jnp.take_along_axis(all_context, row_slots[:, :, None], axis=1)
    all_rows = all_mod.reshape(n_wide * 4, 6 * size)
    grad_bias_ada = jnp.sum(all_rows.astype(F32), axis=0)
    grad_ada = jnp.einsum("sc,sm->cm", rows_context.reshape(-1, cond), all_rows, preferred_element_type=F32)
    own_rows = lax.dynamic_index_in_dim(all_mod.reshape(n_wide, 4, 6 * size), w, 0, False)
    own_row_slots = jnp.stack([own_slot, own_slot, (own_slot + 1) % slots, (own_slot + 2) % slots])
    placed = (own_row_slots[None, :] == jnp.arange(slots)[:, None]).astype(BF16)
    mod_low = jnp.dot(placed, own_rows, preferred_element_type=F32).astype(BF16)
    grad_context = jnp.einsum("sm,cm->sc", mod_low, w_ada, preferred_element_type=F32)
    _, silu_back = jax.vjp(jax.nn.silu, time_embed)
    time_grad = silu_back(grad_context)[0]
    g_attn = g_own[0].astype(F32)
    grad_qkv = jnp.swapaxes(g_attn[: 3 * quarter].reshape(3, quarter, size), 1, 2)
    return (
        final_output,
        final_input_grad,
        time_grad,
        grad_qkv,
        g_attn[3 * quarter :],
        g_own[1].astype(F32),
        grad_bias_up,
        g_own[2].astype(F32),
        grad_bias_down,
        grad_gain_one,
        grad_gain_two,
        grad_ada,
        grad_bias_ada,
    )


def solution(mesh):
    return jax.shard_map(
        functools.partial(body, mesh.shape["wide"]),
        mesh=mesh,
        in_specs=(
            P("wide", "narrow"),
            P("wide", None),
            P("wide", None),
            P(None, None, "narrow"),
            P("narrow", None),
            P(None, "narrow"),
            P("narrow"),
            P("narrow", None),
            P(),
            P(),
            P(),
            P(),
            P(),
            P("wide", "narrow"),
        ),
        out_specs=(
            P("wide", "narrow"),
            P("wide", "narrow"),
            P("wide", None),
            P(None, None, "narrow"),
            P("narrow", None),
            P(None, "narrow"),
            P("narrow"),
            P("narrow", None),
            P(),
            P(),
            P(),
            P(),
            P(),
        ),
        check_vma=False,
    )
```

time: 804 us -> 626 us (0.78)
  waiting for transfers between devices: 498 us -> 0.01 us
  Pallas kernels: 0 us -> 248 us
  local copies, waits for them, and re-layouts: 28.8 us -> 88.9 us
  blocking collectives: 28.1 us -> 88.2 us
  matrix products: 158 us -> 101 us
  other arithmetic: 63.7 us -> 79.3 us
    psum x4 -> x0, waiting for transfers between devices: 421 us -> none  [the longest x1 155 us: body(): lax.psum(feed_partial.astype(jnp.bfloat16), 'narrow').astype(jnp.float32)]
    pallas_call x0 -> x2, Pallas kernels: none -> 248 us  [the longest x1 128 us: gather_all(): pl.pallas_call(gather_kernel, out_shape=(jax.ShapeDtypeStruct((2, 4, rows...]
    all_gather x0 -> x2, blocking collectives: none -> 88.2 us  [the longest x1 79.4 us: body(): gathered = lax.all_gather(message, ('wide', 'narrow'))]
    all_gather x2 -> x0, waiting for transfers between devices: 75.9 us -> none  [the longest x1 46.6 us: body(): lax.all_gather(block_input, 'narrow', axis=1, tiled=True)]
    dot_general x41 -> x19, matrix products: 137 us -> 66.4 us  [the longest x1 6.64 us: body(): jnp.einsum('hqk,khd->qhd', low_probs, values, preferred_element_type=F32)]
    psum x1 -> x0, blocking collectives: 28.1 us -> none  [body(): lax.psum((grad_qkv, grad_out, grad_up, grad_bias_up, grad_down, grad_bias...]
    convert_element_type x0 -> x5, local copies, waits for them, and re-layouts: none -> 20.7 us  [the longest x2 7.93 us: body(): (normed_one * gain_one * (1.0 + scale_one) + shift_one).astype(BF16)]
    reshape x0 -> x8, local copies, waits for them, and re-layouts: none -> 15 us  [the longest x2 5 us: split(): return jnp.swapaxes(rows.astype(BF16).reshape(half, 4, own_width), 0, 1)]
  transfers between devices with their start and end apart: 6 -> 4, of which waited for: 6 -> 0; matrix products, arithmetic and copies ran while one was open for 9% -> 13% of each run, Pallas kernels for 0% -> 0%
where the time goes in v1:
time: 626 us; the launch traced here: 616 us
  Pallas kernels  248 us (40%)
  matrix products  101 us (16%)
  local copies, waits for them, and re-layouts  88.9 us (14%)
  blocking collectives  88.2 us (14%)
  other arithmetic  79.3 us (13%)
  between operations  9.38 us (1%)
    pallas_call x1, Pallas kernels, gather_all(): pl.pallas_call(gather_kernel, out_shape=(jax.ShapeDtypeStruct((2, 4, rows...  128 us
    pallas_call x1, Pallas kernels, reduce_all(): pl.pallas_call(functools.partial(reduce_kernel, n_wide, sub), out_shape=(...  119 us
    all_gather x1, blocking collectives, body(): gathered = lax.all_gather(message, ('wide', 'narrow'))  79.4 us
    dot_general x6, matrix products, body(): jnp.einsum('rs,rd->sd', slot_table, piece_grad, precision=highest)  21.5 us
    unnamed x230, local copies, waits for them, and re-layouts  19.3 us
  transfers between devices with their start and end apart: 4, of which 0 were waited for; matrix products, arithmetic and copies ran while one was open for 13% of the time, Pallas kernels for 0%

profile of v1, /device:TPU:0, one launch (start us, length us, event | category | flops | bytes accessed | tf_op | source)
XLA Modules:
  0.0 616.3 jit_solution(1683421882084240107)
XLA Ops:
  19.6 128.4 %gather_all.1 = (bf16[2,4,384,192]{3,2,1,0:T(8,128)(2,1)}, bf16[2,4,384,192]{3,2,1,0:T(8,128)(2,1)}, bf16[3,2,768,768]{3,2,1,0:T(8,128)(2,1)}, f32[4,8,128]{2,1,0:T(8,128)}, f32[8,128]{1,0:T(8,128)}) custom-call(bf16[1536,192]{1,0:T(8,128)(2,1)} %fusion.94.x, bf16[1536,192]{1,0:T(8,128)(2,1)} %fusion.93.dy, bf16[768,768]{1,0:T(8,128)(2,1)} %pad_maximum_fusion.2.w_attn, ...), custom_call_target="tpu_custom_call" | custom-call | tf_op jit(solution)/shard_map/gather_all/pallas_call | solution.py:210
  161.9 3.9 copy.157
  165.8 4.1 reshape.739
  179.7 11.2 %fusion.159 = (f32[6,768]{1,0:T(8,128)S(1)}, f32[6,768,768]{1,2,0:T(8,128)}) fusion(pred[768,768]{0,1:T(8,128)(4,1)} %broadcast_compare_fusion, bf16[768,6,32]{0,2,1:T(8,128)(2,1)} %get-tuple-element.78, bf16[768,6,32]{0,2,1:T(8,128)(2,1)} %get-tuple-element.79, f32[768,6,32]{0,2,1:T(8,128)} %get-tuple-element.73, f32[768,6,32]{0,2,1:T(8,128)S(1)} %get-tuple-element.72), kind=kOutput, calls=%fused_computation.260 | convolution fusion | flops 465666816 | bytes 16533504 | tf_op jit(solution)/shard_map/sub | solution.py:627
  190.8 6.6 %fusion.55 = bf16[6,64,768]{2,1,0:T(8,128)(2,1)S(1)} fusion(bf16[768,6,64]{0,2,1:T(8,128)(2,1)} %bitcast.222, f32[6,768,768]{1,2,0:T(8,128)} %get-tuple-element.90, f32[6,768]{1,0:T(8,128)S(1)} %get-tuple-element.89), kind=kOutput, calls=%fused_computation.107 | convolution fusion | flops 460357632 | bytes 15353856 | tf_op jit(solution)/shard_map/hqk,khd->qhd/dot_general | solution.py:631
  200.4 4.9 fusion.155
  209.3 8.9 %all-gather.2 = f32[8,4,128]{2,1,0:T(4,128)S(1)} all-gather(f32[1,4,128]{2,1,0:T(4,128)S(1)} %maximum_bitcast_fusion.2), channel_id=2, replica_groups=mesh['wide'=8,'narrow'=4] {'wide'}, dimensions={0}, use_global_device_ids=true | all-gather | bytes 18432 | tf_op jit(solution)/shard_map/all_gather | solution.py:722
  226.9 4.5 copy.156
  233.2 3.9 copy.161
  239.6 4.5 copy.159
  259.6 5.3 fusion.21
  264.9 6.4 %fusion.151 = (bf16[1536]{0:T(1024)(128)(2,1)}, bf16[768,1536]{1,0:T(8,128)(2,1)}) fusion(f32[768,1536]{1,0:T(8,128)S(1)} %get-tuple-element.92, f32[1536]{0:T(1024)S(1)} %copy-done.97, bf16[768,768]{0,1:T(8,128)(2,1)S(1)} %bitcast.216, bf16[1536,768]{1,0:T(8,128)(2,1)S(1)} %bitcast.209), kind=kOutput, calls=%fused_computation.254 | convolution fusion | flops 1837890048 | bytes 10626048 | tf_op jit(solution)/shard_map/rd,fd->rf/dot_general | solution.py:654
  271.4 4.5 copy.206
  275.9 5.6 bitcast_convert_fusion.1
  285.6 4.3 copy.200
  291.3 6.4 %convert_bitcast_fusion.3 = bf16[1,2,768,768]{3,2,1,0:T(8,128)(2,1)} fusion(bf16[768,2,768]{0,2,1:T(8,128)(2,1)} %bitcast.205, f32[768,768]{0,1:T(8,128)} %copy-done.1, f32[768]{0:T(1024)} %get-tuple-element.51, f32[768]{0:T(1024)} %get-tuple-element.52, f32[768]{0:T(1024)} %get-tuple-element.42, f32[768]{0:T(1024)} %get-tuple-element.43, f32[768]{0:T(1024)} %param.24, ...), kind=kOutput, calls=%fused_computation.70 | convolution fusion | flops 1818427392 | bytes 7100160 | tf_op jit(solution)/shard_map/rd,rqf->qdf/dot_general | solution.py:658
  305.3 8.9 %add_convert_fusion.2 = (bf16[768,768]{0,1:T(8,128)(2,1)}, f32[768,768]{0,1:T(8,128)S(1)}) fusion(f32[768,768]{0,1:T(8,128)S(1)} %copy-done.2, bf16[768,768]{0,1:T(8,128)(2,1)S(1)} %collective-permute-done.2, bf16[768,768]{0,1:T(8,128)(2,1)S(1)} %copy-done.14, f32[768]{0:T(1024)S(1)} %copy-done.84, f32[768]{0:T(1024)S(1)} %copy-done.69, ...), kind=kLoop, calls=%fused_computation.67 | loop fusion | flops 12976128 | bytes 13007616 | tf_op jit(solution)/shard_map/convert_element_type | solution.py:647
  318.9 6.3 %multiply_reduce_fusion = (f32[6,768]{1,0:T(8,128)S(1)}, f32[6,768,768]{1,2,0:T(8,128)}) fusion(f32[6,768,768]{1,2,0:T(8,128)S(1)} %bitcast.189, f32[6,768]{1,0:T(8,128)S(1)} %copy-done.81, bf16[768,6,64]{0,2,1:T(8,128)(2,1)S(1)} %bitcast.237, bf16[768,6,64]{0,2,1:T(8,128)(2,1)S(1)} %bitcast.223), kind=kOutput, calls=%fused_computation.3 | convolution fusion | flops 463597056 | bytes 29528064 | tf_op jit(solution)/shard_map/qhd,khd->hqk/dot_general | solution.py:669
  325.1 6.4 %multiply_convert_fusion = bf16[6,768,768]{1,2,0:T(8,128)(2,1)S(1)} fusion(f32[6,768,768]{1,2,0:T(8,128)} %get-tuple-element.94, f32[6,768]{1,0:T(8,128)S(1)} %get-tuple-element.93, f32[6,768,768]{1,2,0:T(8,128)S(1)} %bitcast.189, f32[6,768]{1,0:T(8,128)S(1)} %copy-done.81), kind=kLoop, calls=%fused_computation.2 | loop fusion | flops 14155776 | bytes 35426304 | tf_op jit(solution)/shard_map/convert_element_type | solution.py:671
  354.9 3.9 multiply_reduce_fusion.3
  364.6 119.2 %reduce_all.1 = (bf16[3,4,192,768]{3,2,1,0:T(8,128)(2,1)}, bf16[4,384,192]{2,1,0:T(8,128)(2,1)}, bf16[4,384,192]{2,1,0:T(8,128)(2,1)}) custom-call(bf16[3,2,768,768]{3,2,1,0:T(8,128)(2,1)} %pad_maximum_fusion.grads, bf16[4,768,192]{2,1,0:T(8,128)(2,1)} %bitcast.193, bf16[4,768,192]{2,1,0:T(8,128)(2,1)} %bitcast.194), custom_call_target="tpu_custom_call" | custom-call | tf_op jit(solution)/shard_map/reduce_all/pallas_call | solution.py:475
  493.4 4.1 fusion.81
  505.0 4.1 fusion.87
  512.4 79.4 %all-gather.1 = bf16[32,1,7296]{2,1,0:T(2,128)(2,1)S(1)} all-gather(bf16[1,1,7296]{2,1,0:T(2,128)(2,1)S(1)} %maximum_bitcast_fusion.1), channel_id=1, replica_groups=mesh['wide'=8,'narrow'=4] {'wide','narrow'}, dimensions={0}, use_global_device_ids=true | all-gather | bytes 481536 | tf_op jit(solution)/shard_map/all_gather | solution.py:691
  (364 shorter events, 161.6 us)
Async XLA Ops:
  0.6 155.0 %copy-start = (bf16[128,4608]{1,0:T(8,128)(2,1)S(1)}, bf16[128,4608]{1,0:T(8,128)(2,1)}, u32[]{:S(2)}) copy-start(bf16[128,4608]{1,0:T(8,128)(2,1)} %param.25) | copy-start | bytes 3538948
  7.4 8.5 %copy-start.102 = (f32[768]{0:T(1024)S(1)}, f32[768]{0:T(1024)}, u32[]{:S(2)}) copy-start(f32[768]{0:T(1024)} %param.20) | copy-start | bytes 9220
  7.4 9.1 %copy-start.44 = (bf16[192,768]{1,0:T(8,128)(2,1)S(1)}, bf16[192,768]{1,0:T(8,128)(2,1)}, u32[]{:S(2)}) copy-start(bf16[192,768]{1,0:T(8,128)(2,1)} %param.18) | copy-start | bytes 884740
  148.0 7.6 %copy-start.83 = (f32[4608]{0:T(1024)S(1)}, f32[4608]{0:T(1024)}, u32[]{:S(2)}) copy-start(f32[4608]{0:T(1024)} %param.26) | copy-start | bytes 55300
  152.7 23.5 %copy-start.62 = (pred[768]{0:T(1024)(128)(4,1)}, pred[768]{0:T(1024)(128)(4,1)S(1)}, u32[]{:S(2)}) copy-start(pred[768]{0:T(1024)(128)(4,1)S(1)} %iota_compare_fusion) | copy-start | bytes 2308
  179.7 11.2 %copy-start.22 = (f32[768,6,32]{0,2,1:T(8,128)}, f32[768,6,32]{0,2,1:T(8,128)S(1)}, u32[]{:S(2)}) copy-start(f32[768,6,32]{0,2,1:T(8,128)S(1)} %get-tuple-element.72) | copy-start | bytes 1769476
  190.8 6.7 %copy-start.27 = (bf16[1,2,192,768]{3,2,1,0:T(8,128)(2,1)S(1)}, bf16[1,2,192,768]{3,2,1,0:T(8,128)(2,1)}, u32[]{:S(2)}) copy-start(bf16[1,2,192,768]{3,2,1,0:T(8,128)(2,1)} %slice.174) | copy-start | bytes 1769476
  199.3 55.4 %collective-permute-start = (bf16[768,768]{0,1:T(8,128)(2,1)}, bf16[768,768]{0,1:T(8,128)(2,1)}, u32[]{:S(2)}, u32[]{:S(2)}) collective-permute-start(bf16[768,768]{0,1:T(8,128)(2,1)} %convolution_convert_fusion.1), channel_id=1, source_target_pairs={{0,4},{4,0},{8,12},{12,8},{16,20},{20,16},{24,28},{28,24},{1,5},{5... | collective-permute-start | bytes 3538952 | tf_op jit(solution)/shard_map/ppermute | solution.py:636
  207.3 17.2 %copy-start.10 = (bf16[2,768,768]{1,2,0:T(8,128)(2,1)S(1)}, bf16[2,768,768]{1,2,0:T(8,128)(2,1)}, u32[]{:S(2)}) copy-start(bf16[2,768,768]{1,2,0:T(8,128)(2,1)} %get-tuple-element.58) | copy-start | bytes 7077892
  257.0 7.9 %copy-start.1 = (f32[768,768]{0,1:T(8,128)}, f32[768,768]{0,1:T(8,128)S(1)}, u32[]{:S(2)}) copy-start(f32[768,768]{0,1:T(8,128)S(1)} %get-tuple-element.56) | copy-start | bytes 7077892
  257.4 7.5 %copy-start.53 = (f32[768]{0:T(1024)}, f32[768]{0:T(1024)S(1)}, u32[]{:S(2)}) copy-start(f32[768]{0:T(1024)S(1)} %add_rsqrt_fusion) | copy-start | bytes 9220
  281.4 19.9 %collective-permute-start.1 = (bf16[768,768]{0,1:T(8,128)(2,1)}, bf16[768,768]{0,1:T(8,128)(2,1)}, u32[]{:S(2)}, u32[]{:S(2)}) collective-permute-start(bf16[768,768]{0,1:T(8,128)(2,1)} %bitcast_convert_fusion.1), channel_id=1, source_target_pairs={{0,4},{4,0},{8,12},{12,8},{16,20},{20,16},{24,28},{28,24},{1,5},{5... | collective-permute-start | bytes 3538952 | tf_op jit(solution)/shard_map/ppermute | solution.py:636
  289.8 15.3 %collective-permute-start.2 = (bf16[768,768]{0,1:T(8,128)(2,1)}, bf16[768,768]{0,1:T(8,128)(2,1)S(1)}, u32[]{:S(2)}, u32[]{:S(2)}) collective-permute-start(bf16[768,768]{0,1:T(8,128)(2,1)} %fusion.49), channel_id=1, source_target_pairs={{0,4},{4,0},{8,12},{12,8},{16,20},{20,16},{24,28},{28,24},{1,5},{5... | collective-permute-start | bytes 3538952 | tf_op jit(solution)/shard_map/ppermute | solution.py:636
  291.3 25.2 %slice-start = ((s8[14155776]{0:T(1024)(128)(4,1)}), s8[4194304]{0:T(1024)(128)(4,1)S(1)}, s32[]{:S(2)}) async-start(s8[14155776]{0:T(1024)(128)(4,1)} %bitcast.188), calls=%async_computation | async-start | bytes 8388608
  291.3 25.2 %slice-start.1 = ((s8[14155776]{0:T(1024)(128)(4,1)}), s8[4194304]{0:T(1024)(128)(4,1)S(1)}, s32[]{:S(2)}) async-start(s8[14155776]{0:T(1024)(128)(4,1)} %bitcast.188), calls=%async_computation.1 | async-start | bytes 8388608
  297.8 18.7 %slice-start.2 = ((s8[14155776]{0:T(1024)(128)(4,1)}), s8[4194304]{0:T(1024)(128)(4,1)S(1)}, s32[]{:S(2)}) async-start(s8[14155776]{0:T(1024)(128)(4,1)} %bitcast.188), calls=%async_computation.2 | async-start | bytes 8388608
  305.2 9.0 %copy-start.16 = (bf16[768,768]{0,1:T(8,128)(2,1)}, bf16[768,768]{0,1:T(8,128)(2,1)S(1)}, u32[]{:S(2)}) copy-start(bf16[768,768]{0,1:T(8,128)(2,1)S(1)} %collective-permute-done.2) | copy-start | bytes 3538948
  305.2 10.4 %copy-start.28 = (bf16[1,2,192,768]{3,2,1,0:T(8,128)(2,1)S(1)}, bf16[1,2,192,768]{3,2,1,0:T(8,128)(2,1)}, u32[]{:S(2)}) copy-start(bf16[1,2,192,768]{3,2,1,0:T(8,128)(2,1)} %slice.174) | copy-start | bytes 1769476
  305.2 10.4 %copy-start.86 = (f32[768]{0:T(1024)S(1)}, f32[768]{0:T(1024)}, u32[]{:S(2)}) copy-start(f32[768]{0:T(1024)} %get-tuple-element.45) | copy-start | bytes 9220
  305.2 10.4 %copy-start.87 = (f32[768]{0:T(1024)S(1)}, f32[768]{0:T(1024)}, u32[]{:S(2)}) copy-start(f32[768]{0:T(1024)} %get-tuple-element.46) | copy-start | bytes 9220
  305.2 11.3 %slice-start.3 = ((s8[14155776]{0:T(1024)(128)(4,1)}), s8[1572864]{0:T(1024)(128)(4,1)S(1)}, s32[]{:S(2)}) async-start(s8[14155776]{0:T(1024)(128)(4,1)} %bitcast.188), calls=%async_computation.3 | async-start | bytes 3145728
  340.0 14.8 %collective-permute-start.3 = (bf16[768,768]{0,1:T(8,128)(2,1)}, bf16[768,768]{0,1:T(8,128)(2,1)}, u32[]{:S(2)}, u32[]{:S(2)}) collective-permute-start(bf16[768,768]{0,1:T(8,128)(2,1)} %bitcast_convert_fusion), channel_id=1, source_target_pairs={{0,4},{4,0},{8,12},{12,8},{16,20},{20,16},{24,28},{28,24},{1,5},{5... | collective-permute-start | bytes 3538952 | tf_op jit(solution)/shard_map/ppermute | solution.py:636
  598.4 10.2 %copy-start.18 = (bf16[1,4,192,768]{3,2,1,0:T(8,128)(2,1)S(1)}, bf16[1,4,192,768]{3,2,1,0:T(8,128)(2,1)}, u32[]{:S(2)}) copy-start(bf16[1,4,192,768]{3,2,1,0:T(8,128)(2,1)} %get-tuple-element.59) | copy-start | bytes 3538948
  598.4 10.2 %copy-start.19 = (bf16[1,4,192,768]{3,2,1,0:T(8,128)(2,1)S(1)}, bf16[1,4,192,768]{3,2,1,0:T(8,128)(2,1)}, u32[]{:S(2)}) copy-start(bf16[1,4,192,768]{3,2,1,0:T(8,128)(2,1)} %get-tuple-element.60) | copy-start | bytes 3538948
  (92 other events, 329.4 us)

commit v2 on v0

v2 whole, which is shorter than its diff:
```python
import functools
from types import SimpleNamespace

import jax
import jax.numpy as jnp
from jax import lax
from jax.experimental import pallas as pl
from jax.experimental.pallas import tpu as pltpu
from jax.sharding import PartitionSpec as P

HD = 64
LOG2_E = 1.4426950408889634
epsilon = 1e-05
MESH = pl.DeviceIdType.MESH
CHUNKS = 3
F32 = jnp.float32
BF16 = jnp.bfloat16


def flip(w, bit, step):
    return w + step * (1 - 2 * bit)


def remote(src, dst, send, recv, device):
    return pltpu.make_async_remote_copy(
        src_ref=src, dst_ref=dst, send_sem=send, recv_sem=recv, device_id=device, device_id_type=MESH
    )


def landed(ref, sem):
    pltpu.make_async_copy(ref, ref, sem).wait()


def dot(a, b, dims):
    return lax.dot_general(a, b, (dims, ((), ())), preferred_element_type=F32)


def nn(a, b):
    return dot(a, b, ((1,), (0,)))


def nt(a, b):
    return dot(a, b, ((1,), (1,)))


def tn(a, b):
    return dot(a, b, ((0,), (0,)))


TILE = 256


def tiles(count, step, size=TILE):
    def run(i, carry):
        step(pl.ds(pl.multiple_of(i * size, size), size), i * size)
        return carry

    lax.fori_loop(0, count // size, run, 0)


def norm_stats(inputs):
    row_mean = jnp.mean(inputs, axis=-1, keepdims=True)
    centered = inputs - row_mean
    variance = jnp.mean(centered * centered, axis=-1, keepdims=True)
    scaled = lax.rsqrt(variance + epsilon)
    return (centered * scaled, scaled)


def norm_back(grad_normed, normed, scaled):
    first_term = jnp.mean(grad_normed, axis=-1, keepdims=True)
    second_term = jnp.mean(grad_normed * normed, axis=-1, keepdims=True)
    return scaled * (grad_normed - first_term - normed * second_term)


GAIN_ONE, SHIFT_ONE, GATE_ONE, GAIN_TWO, SHIFT_TWO, GATE_TWO, RISE_ONE, RISE_TWO = range(8)
SUM_G1, SUM_G1N, SUM_GATE_ONE, SUM_G2, SUM_G2N, SUM_GATE_TWO, SUM_DY = range(7)


def chosen(mods, first, piece):
    return jnp.where(first, mods[piece : piece + 1, :], mods[8 + piece : 9 + piece, :])


def first_rows(bound, start, count):
    return (lax.broadcasted_iota(jnp.int32, (count, 1), 0) + start).astype(F32) < bound


def add_sums(sums, piece, first, values):
    total = jnp.sum(values, axis=0, keepdims=True)
    head = jnp.sum(jnp.where(first, values, 0.0), axis=0, keepdims=True)
    sums[piece : piece + 1, :] += head
    sums[8 + piece : 9 + piece, :] += total - head


def swapped(pair):
    lane = lax.broadcasted_iota(jnp.int32, pair.shape, 1)
    return jnp.where(lane % HD < HD // 2, pltpu.roll(pair, 128 - HD // 2, 1), pltpu.roll(pair, HD // 2, 1))


def lanes(g):
    return pl.ds(g * 128, 128)


def head_only(pair, hh):
    lane = lax.broadcasted_iota(jnp.int32, pair.shape, 1)
    return jnp.where((lane < HD) == (hh == 0), pair, jnp.zeros_like(pair))


def project(bound, start, rows, x, mods, cosine, sine, w_attn, in_one, q, k, v):
    s = pl.ds(pl.multiple_of(start, 64), rows)
    first = first_rows(bound, start, rows)
    normed, _ = norm_stats(x[s, :].astype(F32))
    low = (normed * chosen(mods, first, GAIN_ONE) + chosen(mods, first, SHIFT_ONE)).astype(BF16)
    in_one[s, :] = low
    cos_rows, sin_rows = cosine[s, :], sine[s, :]
    for t, target in enumerate((q, k)):
        raw = nt(low, w_attn[t])
        for g in range(raw.shape[1] // 128):
            pair = raw[:, g * 128 : (g + 1) * 128]
            turned = pair * cos_rows + swapped(pair) * sin_rows
            target[s, lanes(g)] = (turned * (0.125 * LOG2_E if t == 0 else 1.0)).astype(BF16)
    v[s, :] = nt(low, w_attn[2]).astype(BF16)


def attend(bound, g, q, k, v, probs, scales, mixed):
    rows = q.shape[0]

    def step(s, start):
        first = first_rows(bound, start, TILE)
        column = lax.broadcasted_iota(jnp.int32, (1, rows), 1).astype(F32) < bound
        bias = jnp.where(first == column, 0.0, -1e30)
        halves = []
        for hh in range(2):
            scores = nt(head_only(q[s, lanes(g)], hh), k[:, lanes(g)]) + bias
            expos = jnp.exp2(scores - jnp.max(scores, axis=-1, keepdims=True))
            low = expos.astype(BF16)
            probs[2 * g + hh, s, :] = low
            scale = 1.0 / jnp.sum(expos, axis=-1, keepdims=True)
            kept = scales[s, :]
            scales[s, :] = jnp.where(lax.broadcasted_iota(jnp.int32, kept.shape, 1) == 2 * g + hh, scale, kept)
            halves.append(nn(low, v[:, lanes(g)]) * scale)
        lane = lax.broadcasted_iota(jnp.int32, halves[0].shape, 1)
        mixed[s, lanes(g)] = jnp.where(lane < HD, halves[0], halves[1]).astype(BF16)

    tiles(rows, step)


def mix_out(mixed, w_attn, part, share):
    def step(s, start):
        part[0, s, :] = nn(mixed[s, :], w_attn[3]).astype(BF16)
        share(s, start)

    tiles(mixed.shape[0], step)


def both(part, s):
    return part[0, s, :].astype(F32) + part[1, s, :].astype(F32)


def hidden_rows(first, s, x, mods, attn_part):
    return x[s, :].astype(F32) + chosen(mods, first, GATE_ONE) * both(attn_part, s)


def feed_up(bound, x, mods, attn_part, w_up, b_up, in_two, act, slope, arrived):
    def step(s, start):
        arrived(s, start)
        first = first_rows(bound, start, TILE)
        normed, _ = norm_stats(hidden_rows(first, s, x, mods, attn_part))
        low = (normed * chosen(mods, first, GAIN_TWO) + chosen(mods, first, SHIFT_TWO)).astype(BF16)
        in_two[s, :] = low
        for n in range(2):
            pre = nn(low, w_up[n]) + b_up[n]
            square = pre * pre
            bent = jnp.tanh(0.7978845608028654 * pre * (1.0 + 0.044715 * square))
            rise = 0.5 * (1.0 + bent)
            act[n, s, :] = (pre * rise).astype(BF16)
            inner = 0.7978845608028654 + 0.10703222443 * square
            slope[n, s, :] = (rise + 0.5 * pre * (1.0 - bent * bent) * inner).astype(BF16)

    tiles(x.shape[0], step)


def feed_grads(bound, dy, mods, feed_low, sums):
    def step(s, start):
        first = first_rows(bound, start, TILE)
        grads = dy[s, :].astype(F32)
        add_sums(sums, SUM_DY, first, grads)
        feed_low[s, :] = (grads * chosen(mods, first, GATE_TWO)).astype(BF16)

    tiles(dy.shape[0], step)


def feed_down(act, w_down, part, share):
    def step(s, start):
        part[0, s, :] = (nn(act[0, s, :], w_down[0]) + nn(act[1, s, :], w_down[1])).astype(BF16)
        share(s, start)

    tiles(act.shape[1], step)


def feed_out(bound, x, dy, mods, attn_part, feed_part, b_down, out, sums, arrived):
    def step(s, start):
        arrived(s, start)
        first = first_rows(bound, start, TILE)
        rows = both(feed_part, s) + b_down
        out[s, :] = (hidden_rows(first, s, x, mods, attn_part) + chosen(mods, first, GATE_TWO) * rows).astype(BF16)
        add_sums(sums, SUM_GATE_TWO, first, dy[s, :].astype(F32) * rows)

    tiles(dy.shape[0], step)


def feed_back(feed_low, slope, w_up, w_down, bias_up, part, share):
    def step(s, start):
        low = feed_low[s, :]
        total = None
        for n in range(2):
            grad_pre = nt(low, w_down[n]) * slope[n, s, :].astype(F32)
            bias_up[n : n + 1, :] += jnp.sum(grad_pre, axis=0, keepdims=True)
            pre = grad_pre.astype(BF16)
            slope[n, s, :] = pre
            term = nt(pre, w_up[n])
            total = term if total is None else total + term
        part[0, s, :] = total.astype(BF16)
        share(s, start)

    tiles(feed_low.shape[0], step)


def weight_grad(left, right, target):
    def step(s, start):
        target[s, :] = tn(left[:, s], right[...]).astype(BF16)

    size = TILE if left.shape[1] % TILE == 0 else 128
    tiles(left.shape[1], step, size)


def norm_two_back(bound, x, dy, mods, back_part, attn_part, w_attn, grad_one, attn_low, grad_mixed, sums, arrived):
    def step(s, start):
        arrived(s, start)
        first = first_rows(bound, start, TILE)
        grads = both(back_part, s)
        normed, scaled = norm_stats(hidden_rows(first, s, x, mods, attn_part))
        add_sums(sums, SUM_G2, first, grads)
        add_sums(sums, SUM_G2N, first, grads * normed)
        rows = dy[s, :].astype(F32) + norm_back(grads * chosen(mods, first, GAIN_TWO), normed, scaled)
        grad_one[s, :] = rows
        add_sums(sums, SUM_GATE_ONE, first, rows * both(attn_part, s))
        low = (rows * chosen(mods, first, GATE_ONE)).astype(BF16)
        attn_low[s, :] = low
        grad_mixed[s, :] = nt(low, w_attn[3]).astype(BF16)

    tiles(dy.shape[0], step)


def attend_back(g, q, k, v, probs, scales, mixed, grad_mixed, cosine, sine, total_k, total_v, grad_q, grad_k, grad_v):
    rows = q.shape[0]

    def turned_back(pair, s):
        return pair * cosine[s, :] - swapped(pair) * sine[s, :]

    total_k[...] = jnp.zeros_like(total_k)
    total_v[...] = jnp.zeros_like(total_v)

    def step(s, start):
        upstream = grad_mixed[s, lanes(g)]
        product = upstream.astype(F32) * mixed[s, lanes(g)].astype(F32)
        halves = []
        for hh in range(2):
            kept = scales[s, :]
            here = lax.broadcasted_iota(jnp.int32, kept.shape, 1) == 2 * g + hh
            scale = jnp.sum(jnp.where(here, kept, 0.0), axis=-1, keepdims=True)
            row_dot = jnp.sum(head_only(product, hh), axis=-1, keepdims=True) * scale
            up_head = (head_only(upstream, hh).astype(F32) * scale).astype(BF16)
            low = probs[2 * g + hh, s, :]
            grad_weights = nt(up_head, v[:, lanes(g)])
            grad_scores = (low.astype(F32) * (grad_weights - row_dot)).astype(BF16)
            halves.append(nn(grad_scores, k[:, lanes(g)]))
            total_v[...] += tn(low, up_head)
            total_k[...] += tn(grad_scores, head_only(q[s, lanes(g)], hh))
        lane = lax.broadcasted_iota(jnp.int32, halves[0].shape, 1)
        pair = jnp.where(lane < HD, halves[0], halves[1]) * 0.125
        grad_q[s, lanes(g)] = turned_back(pair, s).astype(BF16)

    tiles(rows, step)

    def finish(s, start):
        grad_k[s, lanes(g)] = turned_back(total_k[s, :] * (1.0 / LOG2_E), s).astype(BF16)
        grad_v[s, lanes(g)] = total_v[s, :].astype(BF16)

    tiles(rows, finish)


def project_back(grad_q, grad_k, grad_v, w_attn, part, share):
    def step(s, start):
        total = nn(grad_q[s, :], w_attn[0]) + nn(grad_k[s, :], w_attn[1]) + nn(grad_v[s, :], w_attn[2])
        part[0, s, :] = total.astype(BF16)
        share(s, start)

    tiles(grad_q.shape[0], step)


def norm_one_back(bound, x, mods, back_part, grad_one, in_grad, sums, arrived):
    def step(s, start):
        arrived(s, start)
        first = first_rows(bound, start, TILE)
        grads = both(back_part, s)
        normed, scaled = norm_stats(x[s, :].astype(F32))
        add_sums(sums, SUM_G1, first, grads)
        add_sums(sums, SUM_G1N, first, grads * normed)
        rows = grad_one[s, :] + norm_back(grads * chosen(mods, first, GAIN_ONE), normed, scaled)
        in_grad[s, :] = rows.astype(BF16)

    tiles(x.shape[0], step)


ROW_B_UP, ROW_B_DOWN, ROW_GAIN_ONE, ROW_GAIN_TWO, ROW_B_ADA = 0, 1, 2, 3, 8
MSG_MOD, MSG_B_DOWN, MSG_GAIN_ONE, MSG_GAIN_TWO, MSG_B_UP, MSG_CONTEXT = 0, 6, 7, 8, 9, 11
MSG_ROWS = 16


def scratch_plan(n_wide, rows, width, size, cond):
    half, heads = rows // 2, 2 * width // HD
    block = size // 4
    buffers = {
        "raw": ((2, width, rows), BF16),
        "tail": ((half // 2, 128), F32),
        "small": ((16, size), F32),
        "b_all": ((4, 8, size), F32),
        "b_own": ((8, size), F32),
        "info": ((2, 8, 128), F32),
        "context": ((8, 128), F32),
        "mods": ((16, size), F32),
        "sums": ((16, size), F32),
        "bias_up": ((8, size), F32),
        "message": ((MSG_ROWS, size), BF16),
        "rest": ((2, 4, half // 4, 128), BF16),
        "result_rest": ((2, 4, half // 4, 128), BF16),
        "x_low": ((half, size), BF16),
        "dy_low": ((half, size), BF16),
        "cosine": ((half, 128), F32),
        "sine": ((half, 128), F32),
        "w_attn": ((4, 2 * block, size), BF16),
        "w_ff": ((2, 2, size, size), BF16),
        "in_one": ((half, size), BF16),
        "q": ((half, 2 * width), BF16),
        "k": ((half, 2 * width), BF16),
        "v": ((half, 2 * width), BF16),
        "probs": ((heads, half, half), BF16),
        "scales": ((half, 128), F32),
        "mixed": ((half, 2 * width), BF16),
        "attn_part": ((2, half, size), BF16),
        "feed_part": ((2, half, size), BF16),
        "back_part": ((2, half, size), BF16),
        "in_two": ((half, size), BF16),
        "act": ((2, half, size), BF16),
        "slope": ((2, half, size), BF16),
        "out_low": ((half, size), BF16),
        "feed_low": ((half, size), BF16),
        "grad_one": ((half, size), F32),
        "grad_mixed": ((half, 2 * width), BF16),
        "total_k": ((half, 128), F32),
        "total_v": ((half, 128), F32),
        "grad_q": ((half, 2 * width), BF16),
        "grad_k": ((half, 2 * width), BF16),
        "grad_v": ((half, 2 * width), BF16),
        "g_attn": ((4, 2 * block, size), BF16),
        "g_ff": ((2, 2, size, size), BF16),
        "near_half": ((CHUNKS, 2, 2, block // 2, size), BF16),
        "near_full": ((CHUNKS, 2, 2, block, size), BF16),
        "from_z": ((CHUNKS, 3, block, size), BF16),
    }
    planes = n_wide // 2
    groups = n_wide // 8
    semaphores = {
        "load": (26,),
        "msg_load": (n_wide, 4),
        "end_small": (17,),
        "pair": (4,),
        "pair_in": (4,),
        "b_send": (4,),
        "b_in": (4,),
        "x_send": (2, 4, 2),
        "x_in": (2, 4, 2),
        "home": (CHUNKS, 4),
        "home_send": (CHUNKS, 2),
        "edge_send": (CHUNKS, 2),
        "z_in": (CHUNKS, 2),
        "w_send": (CHUNKS, 2, 4),
        "w_in": (CHUNKS, 2, 4),
        "part_send": (4, 4),
        "part_in": (4, 4),
        "out_send": (2, 4, 2),
        "out_in": (2, 4, 2),
        "g_send": (CHUNKS, 2, 5),
        "g_in": (CHUNKS, 2, 4),
        "gz_in": (CHUNKS, 3),
        "group_send": (CHUNKS, groups),
        "group_in": (CHUNKS, groups),
        "group_load": (CHUNKS,),
        "end_send": (CHUNKS, 8),
        "end_in": (CHUNKS, 9),
        "m_send": (5,),
        "m_in": (5,),
        "mp_send": (planes,),
        "mp_in": (planes,),
    }
    return buffers, semaphores


def layer_kernel(n_wide, rows, width, size, cond, slots, *refs):
    buffers, semaphores = scratch_plan(n_wide, rows, width, size, cond)
    names = (
        ["lengths", "x", "dy", "w_qkv", "w_out", "w_up", "w_down", "b_up", "b_down", "gain_one", "gain_two", "w_ada"]
        + ["b_ada", "times", "out_t", "in_t", "out_o", "in_o", "out_r", "in_r", "g_out", "messages", "groups"]
        + ["ada_out", "b_ada_out", "b_down_out", "gain_one_out", "gain_two_out", "b_up_out", "time_out"]
        + list(buffers)
    )
    r = SimpleNamespace(**dict(zip(names, refs)))
    sem = SimpleNamespace(**dict(zip(semaphores, refs[len(names) :])))
    half = rows // 2
    part = half // 2
    block = size // 4
    planes, groups = n_wide // 2, n_wide // 8

    w = lax.axis_index("wide")
    z = lax.axis_index("narrow")
    c, bx, by, plane_at = w % 2, (w // 2) % 2, (w // 4) % 2, w // 2
    pair = (flip(w, c, 1), z)
    next_x, next_y = (flip(w, bx, 2), z), (flip(w, by, 4), z)
    mine = bx + 2 * by
    block_x, block_y, block_d = mine + 1 - 2 * bx, mine + 2 - 4 * by, 3 - mine
    far = [(z - 2 * c - q) % 4 for q in range(2)]
    home = c == z // 2
    odd = z % 2 == 1

    peers = [(w if same else pair[0], (z + dz) % 4) for same in (1, 0) for dz in range(4) if not (same and dz == 0)]
    peers += [((w + 2 * step) % n_wide, z) for step in range(1, planes)]
    barrier = pltpu.get_barrier_semaphore()
    for device in peers:
        pl.semaphore_signal(barrier, inc=1, device_id=device, device_id_type=MESH)

    w_ada = r.probs.at[2]
    loads = [pltpu.make_async_copy(r.x, r.raw.at[0], sem.load.at[0])]
    loads.append(pltpu.make_async_copy(r.dy, r.raw.at[1], sem.load.at[1]))
    for i, ref in enumerate((r.b_up, r.b_down, r.gain_one, r.gain_two)):
        loads.append(pltpu.make_async_copy(ref, r.small.at[i], sem.load.at[2 + i]))
    for i in range(6):
        piece = pl.ds(i * size, size)
        loads.append(pltpu.make_async_copy(r.b_ada.at[piece], r.small.at[ROW_B_ADA + i], sem.load.at[20 + i]))
    for i in range(6):
        loads.append(
            pltpu.make_async_copy(
                r.w_ada.at[:, pl.ds(i * size, size)], w_ada.at[pl.ds(i * cond, cond)], sem.load.at[7 + i]
            )
        )
    for load in loads:
        load.start()
    r.info[0] = jnp.zeros((8, 128), F32)
    time_load = pltpu.make_async_copy(r.times, r.info.at[0, pl.ds(0, slots)], sem.load.at[13])
    time_load.start()

    def w_block(t, q, index, start=0, count=block):
        if t == 0:
            return r.w_attn.at[index, pl.ds(q * block + start, count)]
        return r.w_ff.at[t - 1, q, pl.ds(pl.multiple_of(index * block + start, 32), count)]

    def home_copies(t, q):
        if t == 0:
            copies = [pltpu.make_async_copy(r.w_qkv.at[i], w_block(0, q, i), sem.home.at[0, i]) for i in range(3)]
            return copies + [pltpu.make_async_copy(r.w_out, w_block(0, q, 3), sem.home.at[0, 3])]
        return [pltpu.make_async_copy((r.w_up, r.w_down)[t - 1], r.w_ff.at[t - 1, q], sem.home.at[t, 0])]

    edge, middle = 3 - 3 * c, 2 - c

    def home_sends(t, q, source):
        return [
            remote(
                source, w_block(t, q, mine), sem.home_send.at[t, n], sem.z_in.at[t, q], (w, c + (c + q + n + 1) % 3)
            )
            for n in range(2)
        ]

    def home_each(t, q, action):
        if t == 0:

            @pl.when(mine == 3)
            def _():
                for copy in home_sends(t, q, r.w_out):
                    action(copy)

            @pl.when(mine != 3)
            def _():
                for copy in home_sends(t, q, r.w_qkv.at[jnp.minimum(mine, 2)]):
                    action(copy)

        else:
            for copy in home_sends(t, q, (r.w_up, r.w_down)[t - 1].at[pl.ds(pl.multiple_of(mine * block, 32), block)]):
                action(copy)

    def edge_copy(t, q):
        ref = w_block(t, q, mine)
        return remote(ref, ref, sem.edge_send.at[t, q], sem.z_in.at[t, q], (w, edge))

    def w_copy(t, q, n):
        index, start, count, device = (
            (mine, 0, block, next_x),
            (mine, 0, block, next_y),
            (block_x, 0, block // 2, next_y),
            (block_y, block // 2, block // 2, next_x),
        )[n]
        ref = w_block(t, q, index, start, count)
        return remote(ref, ref, sem.w_send.at[t, q, n], sem.w_in.at[t, q, n], device)

    def weights_start(t):
        for q in range(2):

            @pl.when(far[q] == 0)
            def _():
                home_each(t, q, lambda copy: copy.start())
                for copy in home_copies(t, q):
                    copy.start()

    def weights_own(t):
        for q in range(2):

            @pl.when(far[q] != 0)
            def _():
                landed(w_block(t, q, mine), sem.z_in.at[t, q])

                @pl.when(z == middle)
                def _():
                    edge_copy(t, q).start()

                w_copy(t, q, 0).start()
                w_copy(t, q, 1).start()

    def weights_pass(t):
        for q in range(2):

            @pl.when(far[q] != 0)
            def _():
                landed(w_block(t, q, block_x), sem.w_in.at[t, q, 0])
                w_copy(t, q, 2).start()
                landed(w_block(t, q, block_y), sem.w_in.at[t, q, 1])
                w_copy(t, q, 3).start()

    def weights_done(t):
        for q in range(2):

            @pl.when(far[q] != 0)
            def _():
                landed(w_block(t, q, block_d, 0, block // 2), sem.w_in.at[t, q, 2])
                landed(w_block(t, q, block_d, block // 2, block // 2), sem.w_in.at[t, q, 3])

            @pl.when(far[q] == 0)
            def _():
                for copy in home_copies(t, q):
                    copy.wait()

    def weights_sent(t):
        for q in range(2):

            @pl.when(far[q] == 0)
            def _():
                home_each(t, q, lambda copy: copy.wait_send())

            @pl.when(far[q] != 0)
            def _():
                for n in range(4):
                    w_copy(t, q, n).wait_send()

                @pl.when(z == middle)
                def _():
                    edge_copy(t, q).wait_send()

    stage = (r.probs.at[1], r.g_ff.at[0, 0])
    rests = 2 * 128

    def row_copies(kind, j):
        device = (w - c + j % 2, 2 * c + j // 2)
        own = (c == j % 2) & (2 * c + j // 2 == z)
        target = (r.x_low, r.dy_low)[kind]
        ends = (
            (
                stage[kind].at[pl.ds((j % 2) * part, part), pl.ds((j // 2) * 128, 128)],
                target.at[
                    pl.ds((j % 2) * part, part),
                    pl.ds(pl.multiple_of((z // 2) * (size // 2) + (z % 2) * 256, 128), 128),
                ],
            ),
            (stage[kind].at[pl.ds(j * (part // 2), part // 2), pl.ds(rests, 128)], r.rest.at[kind, z]),
        )
        here = [
            pltpu.make_async_copy(source, dest, sem.x_in.at[kind, z, n]) for n, (source, dest) in enumerate(ends)
        ]
        there = [
            remote(source, dest, sem.x_send.at[kind, j, n], sem.x_in.at[kind, z, n], device)
            for n, (source, dest) in enumerate(ends)
        ]
        return own, here, there

    spans_own = [r.lengths[0, i] for i in range(slots)]
    shift = jnp.where(
        (spans_own[0] >= spans_own[1]) & (spans_own[0] >= spans_own[2]),
        0,
        jnp.where(spans_own[1] >= spans_own[2], spans_own[0], spans_own[0] + spans_own[1]),
    )

    def unit(count, first=0, total=part):
        row = lax.broadcasted_iota(jnp.int32, (count, 1), 0) + first
        column = lax.broadcasted_iota(jnp.int32, (1, total), 1)
        return jnp.where(row == column, 1.0, 0.0).astype(BF16)

    def turn_rows(kind):
        back = jnp.where(shift == 0, 0, rows - shift)
        r.raw[kind] = pltpu.roll(r.raw[kind].astype(F32), back, 1).astype(BF16)
        same = unit(part)
        r.tail[...] = jnp.zeros_like(r.tail)
        for j in range(4):
            turned = nt(same, r.raw[kind, :, j * part : (j + 1) * part])
            main = turned[:, :128]
            r.tail[:, : width - 128] = turned[:, 128:]
            tail = r.tail[...]
            lane = lax.broadcasted_iota(jnp.int32, main.shape, 1)
            main_turned = pltpu.roll(main, 64, 1)
            tail_turned = pltpu.roll(tail, 64, 1)
            full = jnp.where(odd, jnp.where(lane < 64, main_turned, tail_turned), main)
            left = jnp.where(odd, jnp.where(lane < 64, 0.0, main_turned), tail)
            stage[kind][(j % 2) * part : (j % 2 + 1) * part, (j // 2) * 128 : (j // 2 + 1) * 128] = full.astype(BF16)
            packed = left[: part // 2] + pltpu.roll(left[part // 2 :], 64, 1)
            stage[kind][j * (part // 2) : (j + 1) * (part // 2), rests : rests + 128] = packed.astype(BF16)

    def rows_start(kind):
        for j in range(4):
            own, here, there = row_copies(kind, j)

            @pl.when(own)
            def _():
                for copy in here:
                    copy.start()

            @pl.when(jnp.logical_not(own))
            def _():
                for copy in there:
                    copy.start()

    def rows_sent(kind):
        for j in range(4):
            own, _, there = row_copies(kind, j)

            @pl.when(jnp.logical_not(own))
            def _():
                for copy in there:
                    copy.wait_send()

    own_rows = pl.ds(pl.multiple_of(c * part, 128), part)
    other_rows = pl.ds(pl.multiple_of((1 - c) * part, 128), part)

    def pair_rows(kind):
        target = (r.x_low, r.dy_low)[kind]
        return remote(target.at[own_rows], target.at[own_rows], sem.pair.at[kind], sem.pair_in.at[kind], pair)

    def rows_join(kind):
        target = (r.x_low, r.dy_low)[kind]
        for slot in range(4):
            at = (slot // 2) * (size // 2) + (slot % 2) * 256
            landed(target.at[own_rows, pl.ds(at, 128)], sem.x_in.at[kind, slot, 0])
            landed(r.rest.at[kind, slot], sem.x_in.at[kind, slot, 1])
        for g in range(2):
            even, odds = r.rest[kind, 2 * g].astype(F32), r.rest[kind, 2 * g + 1].astype(F32)
            lane = lax.broadcasted_iota(jnp.int32, even.shape, 1)
            upper = jnp.where(lane < 64, even, odds)
            lower = pltpu.roll(jnp.where(lane < 64, odds, even), 64, 1)
            at = pl.ds(g * (size // 2) + 128, 128)
            base = pl.multiple_of(c * part, 128)
            target[pl.ds(base, part // 2), at] = upper.astype(BF16)
            target[pl.ds(base + part // 2, part // 2), at] = lower.astype(BF16)
        pair_rows(kind).start()

    def rows_whole(kind):
        target = (r.x_low, r.dy_low)[kind]
        landed(target.at[other_rows], sem.pair_in.at[kind])

    def part_copy(n, ref, s, start):
        i = start // TILE
        return remote(ref.at[0, s], ref.at[1, s], sem.part_send.at[n, i], sem.part_in.at[n, i], pair)

    def sharing(n, ref):
        return lambda s, start: part_copy(n, ref, s, start).start()

    def arriving(n, ref):
        def wait(s, start):
            copy = part_copy(n, ref, s, start)
            copy.wait_recv()
            copy.wait_send()

        return wait

    def g_block(t, q, index, start=0, count=block):
        if t == 0:
            return r.g_attn.at[index, pl.ds(q * block + start, count)]
        return r.g_ff.at[t - 1, q, pl.ds(pl.multiple_of(index * block + start, 32), count)]

    def add_to(target, terms):
        def step(s, start):
            total = target[s, :].astype(F32)
            for term in terms:
                total = total + term[s, :].astype(F32)
            target[s, :] = total.astype(BF16)

        tiles(target.shape[0], step, 32)

    def g_copy(t, q, n):
        source, dest, device = (
            (g_block(t, q, block_d, 0, block // 2), r.near_half.at[t, q, 0], next_y),
            (g_block(t, q, block_d, block // 2, block // 2), r.near_half.at[t, q, 1], next_x),
            (g_block(t, q, block_x), r.near_full.at[t, q, 0], next_x),
            (g_block(t, q, block_y), r.near_full.at[t, q, 1], next_y),
        )[n]
        return remote(source, dest, sem.g_send.at[t, q, n], sem.g_in.at[t, q, n], device)

    def g_home(t, q, slot):
        return remote(
            g_block(t, q, mine), r.from_z.at[t, slot], sem.g_send.at[t, q, 4], sem.gz_in.at[t, slot], (w, 2 * c + q)
        )

    def g_edge(t, q):
        return remote(g_block(t, q, mine), r.from_z.at[t, q], sem.g_send.at[t, q, 4], sem.gz_in.at[t, q], (w, middle))

    def grads_start(t, q):
        g_copy(t, q, 0).start()
        g_copy(t, q, 1).start()

    def grads_second(t, q):
        g_copy(t, q, 0).wait_recv()
        add_to(g_block(t, q, block_x, 0, block // 2), [r.near_half.at[t, q, 0]])
        g_copy(t, q, 2).start()
        g_copy(t, q, 1).wait_recv()
        add_to(g_block(t, q, block_y, block // 2, block // 2), [r.near_half.at[t, q, 1]])
        g_copy(t, q, 3).start()

    def grads_third(t):
        for q in range(2):
            g_copy(t, q, 2).wait_recv()
            g_copy(t, q, 3).wait_recv()
            add_to(g_block(t, q, mine), [r.near_full.at[t, q, 0], r.near_full.at[t, q, 1]])

            if t == 0:

                @pl.when(far[q] != 0)
                def _():
                    g_home(t, q, far[q] - 1).start()

            else:

                @pl.when(z == edge)
                def _():
                    g_edge(t, q).start()

                @pl.when((far[q] != 0) & (z != edge) & (z != middle))
                def _():
                    g_home(t, q, 0).start()

    def grads_middle(t):
        @pl.when(z == middle)
        def _():
            for q in range(2):
                landed(r.from_z.at[t, q], sem.gz_in.at[t, q])
                add_to(g_block(t, q, mine), [r.from_z.at[t, q]])
                g_home(t, q, 1).start()

    def out_block(t, index, start=0, count=block):
        return r.g_out.at[t, pl.ds(pl.multiple_of(index * block + start, 32), count)]

    def end_local(t, q):
        return pltpu.make_async_copy(g_block(t, q, mine), out_block(t, mine), sem.end_in.at[t, 4])

    def end_copy(t, q, n):
        if n < 2:
            return remote(
                g_block(t, q, mine), out_block(t, mine), sem.end_send.at[t, n], sem.end_in.at[t, n],
                (next_x, next_y)[n],
            )
        ref = out_block(t, block_x, 0, block // 2) if n == 2 else out_block(t, block_y, block // 2, block // 2)
        return remote(ref, ref, sem.end_send.at[t, n], sem.end_in.at[t, n], (next_y, next_x)[n - 2])

    def end_pair(t, n):
        ref = out_block(t, (mine, block_x, block_y, block_d)[n])
        return remote(ref, ref, sem.end_send.at[t, 4 + n], sem.end_in.at[t, 5 + n], pair)

    def group_copy(t, q, step):
        return remote(
            g_block(t, q, mine), r.groups.at[t, step], sem.group_send.at[t, step], sem.group_in.at[t, step],
            ((w + 8 * step) % n_wide, z),
        )

    def grads_fourth(t):
        for q in range(2):

            @pl.when(far[q] == 0)
            def _():
                count = 3 if t == 0 else 2
                for slot in range(count):
                    landed(r.from_z.at[t, slot], sem.gz_in.at[t, slot])
                add_to(g_block(t, q, mine), [r.from_z.at[t, slot] for slot in range(count)])
                for step in range(1, groups):
                    group_copy(t, q, step).start()
                for step in range(1, groups):
                    group_copy(t, q, step).wait()
                for step in range(1, groups):
                    load = pltpu.make_async_copy(r.groups.at[t, step], r.from_z.at[t, 0], sem.group_load.at[t])
                    load.start()
                    load.wait()
                    add_to(g_block(t, q, mine), [r.from_z.at[t, 0]])
                end_local(t, q).start()
                end_copy(t, q, 0).start()
                end_copy(t, q, 1).start()

    def grads_fifth(t):
        for q in range(2):

            @pl.when(far[q] == 0)
            def _():
                landed(out_block(t, block_x), sem.end_in.at[t, 0])
                end_copy(t, q, 2).start()
                end_pair(t, 1).start()
                landed(out_block(t, block_y), sem.end_in.at[t, 1])
                end_copy(t, q, 3).start()
                end_pair(t, 2).start()
                end_local(t, q).wait()
                end_pair(t, 0).start()

    def grads_sixth(t):
        for q in range(2):

            @pl.when(far[q] == 0)
            def _():
                landed(out_block(t, block_d, 0, block // 2), sem.end_in.at[t, 2])
                landed(out_block(t, block_d, block // 2, block // 2), sem.end_in.at[t, 3])
                end_pair(t, 3).start()

    def grads_done(t):
        for q in range(2):
            for n in range(4):
                g_copy(t, q, n).wait_send()

            @pl.when(far[q] != 0)
            def _():
                g_home(t, q, 0).wait_send()

            @pl.when(far[q] == 0)
            def _():
                for n in range(4):
                    end_copy(t, q, n).wait_send()
                for n in range(4):
                    end_pair(t, n).wait_send()

        @pl.when(jnp.logical_not(home))
        def _():
            for index in range(4):
                landed(out_block(t, (mine, block_x, block_y, block_d)[index]), sem.end_in.at[t, 5 + index])

    def result_copies(kind, source, dest):
        window = pl.ds((dest // 2) * (size // 2) + (dest % 2) * 256, 128)
        slot = 2 * (z % 2) + c
        own = home & (z == dest)
        mains, rests_in = ((r.out_o, r.out_r), (r.in_o, r.in_r))[kind]
        ends = (
            (source.at[own_rows, window], mains.at[slot]),
            (r.result_rest.at[kind, dest], rests_in.at[slot]),
        )
        here = [
            pltpu.make_async_copy(ref, target, sem.out_in.at[kind, slot, n]) for n, (ref, target) in enumerate(ends)
        ]
        there = [
            remote(
                ref, target, sem.out_send.at[kind, dest, n], sem.out_in.at[kind, slot, n], (w - c + z // 2, dest)
            )
            for n, (ref, target) in enumerate(ends)
        ]
        return own, here, there

    def results_start(kind, source):
        for g in range(2):
            at = pl.ds(g * (size // 2) + 128, 128)
            base = pl.multiple_of(c * part, 128)
            upper = source[pl.ds(base, part // 2), at].astype(F32)
            lower = pltpu.roll(source[pl.ds(base + part // 2, part // 2), at].astype(F32), 64, 1)
            lane = lax.broadcasted_iota(jnp.int32, upper.shape, 1)
            r.result_rest[kind, 2 * g] = jnp.where(lane < 64, upper, lower).astype(BF16)
            r.result_rest[kind, 2 * g + 1] = jnp.where(lane < 64, lower, upper).astype(BF16)
        for dest in range(4):
            own, here, there = result_copies(kind, source, dest)

            @pl.when(own)
            def _():
                for copy in here:
                    copy.start()

            @pl.when(jnp.logical_not(own))
            def _():
                for copy in there:
                    copy.start()

    def results_done(kind, source):
        mains, rests_in = ((r.out_o, r.out_r), (r.in_o, r.in_r))[kind]
        for slot in range(4):
            landed(mains.at[slot], sem.out_in.at[kind, slot, 0])
            landed(rests_in.at[slot], sem.out_in.at[kind, slot, 1])
        for dest in range(4):
            own, _, there = result_copies(kind, source, dest)

            @pl.when(jnp.logical_not(own))
            def _():
                for copy in there:
                    copy.wait_send()

    def results_turn(kind, stage_at, target, stage_out):
        mains, rests_in = ((r.out_o, r.out_r), (r.in_o, r.in_r))[kind]
        loads = []
        for slot in range(4):
            main_at = stage_at.at[pl.ds((slot // 2) * part, part), pl.ds((slot % 2) * 128, 128)]
            rest_at = stage_at.at[pl.ds(slot * (part // 2), part // 2), pl.ds(256, 128)]
            loads.append(pltpu.make_async_copy(mains.at[slot], main_at, sem.load.at[14 + slot]))
            loads.append(pltpu.make_async_copy(rests_in.at[slot], rest_at, sem.load.at[20 + slot]))
        for load in loads:
            load.start()
        for load in loads:
            load.wait()
        same, upper, lower = unit(part), unit(part // 2), unit(part // 2, part // 2)
        pieces = []
        for slot in range(4):
            main = tn(stage_at[(slot // 2) * part : (slot // 2 + 1) * part, (slot % 2) * 128 : (slot % 2 + 1) * 128], same)
            packed = stage_at[slot * (part // 2) : (slot + 1) * (part // 2), 256:384]
            first, second = tn(packed, upper), tn(packed, lower)
            rest = jnp.where(odd, first[64:] + second[:64], first[:64] + second[64:])
            pieces.append(
                jnp.where(odd, jnp.concatenate([rest, main], axis=0), jnp.concatenate([main, rest], axis=0))
            )
        turned = pltpu.roll(jnp.concatenate(pieces, axis=1), shift, 1).astype(stage_out.dtype)
        stores = []
        for n in range(2):
            stage_out[n * width : (n + 1) * width, :] = turned[:, n * half : (n + 1) * half]
            stores.append(
                pltpu.make_async_copy(
                    stage_out.at[pl.ds(n * width, width)], target.at[:, pl.ds(n * half, half)], sem.load.at[18 + n]
                )
            )
            stores[-1].start()
        for store in stores:
            store.wait()

    w_ada_again = r.slope.at[0]
    ada_loads = [
        pltpu.make_async_copy(
            r.w_ada.at[:, pl.ds(i * size, size)], w_ada_again.at[pl.ds(i * cond, cond)], sem.load.at[7 + i]
        )
        for i in range(6)
    ]

    def finish_small():
        per_slab = half // (4 * MSG_ROWS)
        count = 2 * planes
        slabs = -(-count // per_slab)
        loads = []
        for i in range(count):
            place = r.probs.at[i // per_slab, pl.ds((i % per_slab) * 4 * MSG_ROWS, 4 * MSG_ROWS)]
            source = r.messages.at[i // planes, i % planes]
            loads += [
                pltpu.make_async_copy(source.at[j], place.at[pl.ds(j * MSG_ROWS, MSG_ROWS)], sem.msg_load.at[i, j])
                for j in range(4)
            ]
        for load in loads:
            load.start()
        for load in loads + ada_loads:
            load.wait()
        totals = [None, None]
        ada = [None] * 6
        for n in range(slabs):
            used = min(count - n * per_slab, per_slab) * 4 * MSG_ROWS
            every = r.probs[n, :used, :]
            column = lax.broadcasted_iota(jnp.int32, (MSG_ROWS, used), 1)
            row = lax.broadcasted_iota(jnp.int32, (MSG_ROWS, used), 0)
            early = column + n * half < planes * 4 * MSG_ROWS
            for part_of in range(2):
                wanted = (column % MSG_ROWS == row) & (early if part_of == 0 else jnp.logical_not(early))
                term = nn(jnp.where(wanted, 1.0, 0.0).astype(BF16), every)
                totals[part_of] = term if totals[part_of] is None else totals[part_of] + term
            contexts = every[:, :cond].astype(F32)
            at = lax.broadcasted_iota(jnp.int32, contexts.shape, 0) % MSG_ROWS
            contexts = jnp.where(at == MSG_CONTEXT, contexts, 0.0)
            for i in range(6):
                moved = pltpu.roll(contexts, used - MSG_CONTEXT + i, 0).astype(BF16)
                term = tn(moved, every)
                ada[i] = term if ada[i] is None else ada[i] + term
        for i in range(6):
            r.grad_one[i * cond : (i + 1) * cond, :] = ada[i]
        r.small[...] = totals[0] + totals[1]
        up_rows = jnp.where(z // 2 == 0, totals[0][MSG_B_UP : MSG_B_UP + 2], totals[1][MSG_B_UP : MSG_B_UP + 2])
        r.small[MSG_B_UP : MSG_B_UP + 1, :] = jnp.where(odd, up_rows[1:2], up_rows[0:1])
        own_slot = jnp.where(
            (spans_own[0] >= spans_own[1]) & (spans_own[0] >= spans_own[2]),
            0,
            jnp.where(spans_own[1] >= spans_own[2], 1, 2),
        )
        place = lax.broadcasted_iota(jnp.int32, (8, 1), 0)
        grads = jnp.zeros((8, cond), F32)
        for half_at, seg, after in ((0, 0, 0), (1, 0, 1), (1, 1, 2)):
            group_at = seg * planes + plane_at
            base = (group_at % per_slab) * 4 * MSG_ROWS + (2 * c + half_at) * MSG_ROWS
            rows_at = r.probs[group_at // per_slab, pl.ds(pl.multiple_of(base, MSG_ROWS), MSG_ROWS), :]
            row = lax.broadcasted_iota(jnp.int32, (MSG_ROWS, 1), 0)
            total = jnp.zeros((MSG_ROWS, cond), F32)
            for i in range(6):
                total = total + jnp.where(row == i, nt(rows_at, w_ada_again[i * cond : (i + 1) * cond, :]), 0.0)
            slot = own_slot + after
            slot = jnp.where(slot >= slots, slot - slots, slot)
            grads = grads + jnp.where(place == slot, jnp.sum(total, axis=0, keepdims=True), 0.0)
        times = r.info[0]
        gate = 1.0 / (1.0 + jnp.exp(-times))
        r.context[...] = grads * (gate + times * gate * (1.0 - gate))
        copies = [
            pltpu.make_async_copy(r.grad_one.at[pl.ds(i * cond, cond)], r.ada_out.at[:, pl.ds(i * size, size)], sem.end_small.at[i])
            for i in range(6)
        ]
        copies += [
            pltpu.make_async_copy(r.small.at[i], r.b_ada_out.at[pl.ds(i * size, size)], sem.end_small.at[6 + i])
            for i in range(6)
        ]
        for i, (row, ref) in enumerate(
            ((MSG_B_DOWN, r.b_down_out), (MSG_GAIN_ONE, r.gain_one_out), (MSG_GAIN_TWO, r.gain_two_out), (MSG_B_UP, r.b_up_out))
        ):
            copies.append(pltpu.make_async_copy(r.small.at[row], ref, sem.end_small.at[12 + i]))
        copies.append(pltpu.make_async_copy(r.context.at[pl.ds(0, slots)], r.time_out, sem.end_small.at[16]))
        for copy in copies:
            copy.start()
        return copies

    time_load.wait()
    lane = lax.broadcasted_iota(jnp.int32, (1, 128), 1)
    length_row = jnp.zeros((1, 128), F32)
    for i in range(slots):
        length_row = jnp.where(lane == i, r.lengths[0, i].astype(F32), length_row)
    r.info[0, slots : slots + 1, :] = length_row
    for load in loads[2:6]:
        load.wait()
    r.b_own[...] = r.small[0:8, :]

    pl.semaphore_wait(barrier, len(peers))
    weights_start(0)
    info_copy = remote(r.info.at[0], r.info.at[1], sem.pair.at[2], sem.pair_in.at[2], pair)
    info_copy.start()
    b_copies = [
        remote(r.b_own, r.b_all.at[z], sem.b_send.at[dz], sem.b_in.at[dz], (w, (z + dz) % 4)) for dz in range(1, 4)
    ]
    for copy in b_copies:
        copy.start()
    loads[0].wait()
    turn_rows(0)
    rows_start(0)

    info_copy.wait()
    info = jnp.where(home, r.info[0], r.info[1])
    context = info / (1.0 + jnp.exp(-info))
    context_low = context.astype(BF16)
    spans = [info[slots : slots + 1, i : i + 1] for i in range(slots)]
    longest = [
        (spans[0] >= spans[1]) & (spans[0] >= spans[2]),
        (spans[1] > spans[0]) & (spans[1] >= spans[2]),
        (spans[2] > spans[0]) & (spans[2] > spans[1]),
    ]

    def slot_after(shift):
        return [longest[(i - shift) % slots] for i in range(slots)]

    def pick(flags, values):
        total = None
        for flag, value in zip(flags, values):
            term = jnp.where(flag, value, 0.0)
            total = term if total is None else total + term
        return total

    flags_a = [jnp.where(odd, after.astype(F32), at.astype(F32)) > 0.5 for after, at in zip(slot_after(1), longest)]
    flags_b = [jnp.where(odd, after.astype(F32), at.astype(F32)) > 0.5 for after, at in zip(slot_after(2), longest)]
    bound = jnp.where(odd, pick(slot_after(1), spans), float(half))
    r.context[0:1, :] = pick(flags_a, [context[i : i + 1, :] for i in range(slots)])
    r.context[1:2, :] = pick(flags_b, [context[i : i + 1, :] for i in range(slots)])
    for load in loads[6:]:
        load.wait()
    rises = {}
    for i in range(6):
        modulation = nn(context_low, w_ada[i * cond : (i + 1) * cond, :]) + r.small[ROW_B_ADA + i : ROW_B_ADA + i + 1, :]
        for seg, flags in enumerate((flags_a, flags_b)):
            row = pick(flags, [modulation[n : n + 1, :] for n in range(slots)])
            if i in (1, 4):
                gain = r.small[ROW_GAIN_ONE : ROW_GAIN_ONE + 1, :] if i == 1 else r.small[ROW_GAIN_TWO : ROW_GAIN_TWO + 1, :]
                rise = 8 * seg + (RISE_ONE if i == 1 else RISE_TWO)
                r.mods[rise : rise + 1, :] = 1.0 + row
                row = gain * (1.0 + row)
            at = 8 * seg + (SHIFT_ONE, GAIN_ONE, GATE_ONE, SHIFT_TWO, GAIN_TWO, GATE_TWO)[i]
            r.mods[at : at + 1, :] = row
    inverse = jnp.exp((lane % (HD // 2)).astype(F32) * (-9.210340371976184 / (HD // 2)))
    signs = jnp.where(lane % HD < HD // 2, -1.0, 1.0)

    def tables(s, start):
        row = (lax.broadcasted_iota(jnp.int32, (TILE, 1), 0) + start).astype(F32)
        angles = jnp.where(row < bound, row, row - bound) * inverse
        r.cosine[s, :] = jnp.cos(angles)
        r.sine[s, :] = jnp.sin(angles) * signs

    tiles(half, tables)
    r.scales[...] = jnp.zeros_like(r.scales)
    r.sums[...] = jnp.zeros_like(r.sums)
    r.bias_up[...] = jnp.zeros_like(r.bias_up)
    weights_own(0)
    loads[1].wait()
    turn_rows(1)
    for n, copy in enumerate(b_copies):
        landed(r.b_all.at[(z + 3 - n) % 4], sem.b_in.at[n + 1])
    r.b_all[z] = r.b_own[...]
    weights_pass(0)
    weights_start(1)
    rows_join(0)
    weights_done(0)

    def project_some(i, carry):
        @pl.when(i == 2)
        def _():
            rows_whole(0)

        project(
            bound, ((2 * c + i) % 4) * (part // 2), part // 2, r.x_low, r.mods, r.cosine, r.sine, r.w_attn, r.in_one,
            r.q, r.k, r.v,
        )
        return carry

    lax.fori_loop(0, 4, project_some, 0)
    weights_start(2)
    weights_own(1)
    rows_sent(0)
    attend(bound, 0, r.q, r.k, r.v, r.probs, r.scales, r.mixed)
    weights_pass(1)
    rows_start(1)
    attend(bound, 1, r.q, r.k, r.v, r.probs, r.scales, r.mixed)
    weights_own(2)
    attend(bound, 2, r.q, r.k, r.v, r.probs, r.scales, r.mixed)
    mix_out(r.mixed, r.w_attn, r.attn_part, sharing(0, r.attn_part))
    weights_done(1)
    b_up = jnp.where(c == 0, r.b_all[0, 0:1, :], r.b_all[2, 0:1, :]), jnp.where(c == 0, r.b_all[1, 0:1, :], r.b_all[3, 0:1, :])
    feed_up(
        bound, r.x_low, r.mods, r.attn_part, r.w_ff.at[0], b_up, r.in_two, r.act, r.slope, arriving(0, r.attn_part)
    )
    weights_pass(2)
    rows_join(1)
    rows_whole(1)
    rows_sent(1)
    feed_grads(bound, r.dy_low, r.mods, r.feed_low, r.sums)
    for q in range(2):
        weight_grad(r.act.at[q], r.feed_low, r.g_ff.at[1, q])
        grads_start(2, q)
    weights_done(2)
    feed_down(r.act, r.w_ff.at[1], r.feed_part, sharing(1, r.feed_part))
    grads_second(2, 0)
    feed_back(
        r.feed_low, r.slope, r.w_ff.at[0], r.w_ff.at[1], r.bias_up, r.back_part, sharing(2, r.back_part)
    )
    grads_second(2, 1)
    for q in range(2):
        weight_grad(r.in_two, r.slope.at[q], r.g_ff.at[0, q])
        grads_start(1, q)
    b_down = r.small[ROW_B_DOWN : ROW_B_DOWN + 1, :]
    feed_out(
        bound, r.x_low, r.dy_low, r.mods, r.attn_part, r.feed_part, b_down, r.out_low, r.sums, arriving(1, r.feed_part)
    )
    results_start(0, r.out_low)
    norm_two_back(
        bound, r.x_low, r.dy_low, r.mods, r.back_part, r.attn_part, r.w_attn, r.grad_one, r.feed_low, r.grad_mixed,
        r.sums, arriving(2, r.back_part),
    )
    weight_grad(r.mixed, r.feed_low, r.g_attn.at[3])
    grads_third(2)
    grads_second(1, 0)
    for g in range(3):
        attend_back(
            g, r.q, r.k, r.v, r.probs, r.scales, r.mixed, r.grad_mixed, r.cosine, r.sine, r.total_k, r.total_v,
            r.grad_q, r.grad_k, r.grad_v,
        )
        for t, grads in enumerate((r.grad_q, r.grad_k, r.grad_v)):
            r.g_attn[t, g * 128 : (g + 1) * 128, :] = tn(grads[:, lanes(g)], r.in_one[...]).astype(BF16)
        if g == 0:
            grads_second(1, 1)
        if g == 1:
            grads_start(0, 0)
    grads_start(0, 1)
    grads_third(1)
    project_back(r.grad_q, r.grad_k, r.grad_v, r.w_attn, r.act, sharing(3, r.act))
    grads_second(0, 0)
    grads_second(0, 1)
    grads_middle(2)
    norm_one_back(
        bound, r.x_low, r.mods, r.act, r.grad_one, r.in_two, r.sums, arriving(3, r.act)
    )

    def sum_row(piece):
        return jnp.where(c == 0, r.sums[piece : piece + 1, :], r.sums[8 + piece : 9 + piece, :])

    def mod_row(piece):
        return jnp.where(c == 0, r.mods[piece : piece + 1, :], r.mods[8 + piece : 9 + piece, :])

    gain_one = r.small[ROW_GAIN_ONE : ROW_GAIN_ONE + 1, :]
    gain_two = r.small[ROW_GAIN_TWO : ROW_GAIN_TWO + 1, :]
    context_row = jnp.where(c == 0, r.context[0:1, :], r.context[1:2, :])
    message = [
        sum_row(SUM_G1),
        sum_row(SUM_G1N) * gain_one,
        sum_row(SUM_GATE_ONE),
        sum_row(SUM_G2),
        sum_row(SUM_G2N) * gain_two,
        sum_row(SUM_GATE_TWO),
        sum_row(SUM_DY) * mod_row(GATE_TWO),
        sum_row(SUM_G1N) * mod_row(RISE_ONE),
        sum_row(SUM_G2N) * mod_row(RISE_TWO),
        r.bias_up[0:1, :],
        r.bias_up[1:2, :],
        jnp.concatenate([context_row] + [jnp.zeros((1, 128), F32)] * (size // 128 - 1), axis=1),
        jnp.zeros((4, size), F32),
    ]
    r.message[...] = jnp.concatenate(message, axis=0).astype(BF16)
    message_at = r.messages.at[c, plane_at, z]
    message_local = pltpu.make_async_copy(r.message, message_at, sem.m_in.at[0])
    message_local.start()
    message_copies = [
        remote(r.message, message_at, sem.m_send.at[dz], sem.m_in.at[dz], (w, (z + dz) % 4)) for dz in range(1, 4)
    ]
    for copy in message_copies:
        copy.start()
    for load in ada_loads:
        load.start()
    results_start(1, r.in_two)
    results_done(0, r.out_low)
    results_turn(0, r.act.at[0], r.out_t, r.feed_low)
    grads_middle(1)
    grads_third(0)
    grads_fourth(2)
    grads_fourth(1)
    message_local.wait()
    for dz in range(1, 4):
        landed(r.messages.at[c, plane_at, (z + 4 - dz) % 4], sem.m_in.at[dz])
    plane_copies = []
    for step in range(1, planes):
        ref = r.messages.at[c, plane_at]
        plane_copies.append(
            remote(ref, ref, sem.mp_send.at[step], sem.mp_in.at[step], ((w + 2 * step) % n_wide, z))
        )
        plane_copies[-1].start()
    grads_fifth(2)
    results_done(1, r.in_two)
    results_turn(1, r.act.at[1], r.in_t, r.grad_one)
    for step in range(1, planes):
        landed(r.messages.at[c, (plane_at + planes - step) % planes], sem.mp_in.at[step])
    message_pair = remote(r.messages.at[c], r.messages.at[c], sem.m_send.at[4], sem.m_in.at[4], pair)
    message_pair.start()
    grads_fourth(0)
    grads_fifth(1)
    grads_sixth(2)
    landed(r.messages.at[1 - c], sem.m_in.at[4])
    small_ends = finish_small()
    grads_fifth(0)
    grads_sixth(1)
    grads_sixth(0)
    for copy in small_ends:
        copy.wait()

    for t in range(CHUNKS):
        weights_sent(t)
    for kind in range(2):
        pair_rows(kind).wait_send()
    for copy in b_copies + message_copies + plane_copies + [message_pair]:
        copy.wait_send()
    for t in range(CHUNKS):
        grads_done(t)


def layer(n_wide, lengths, x, *others):
    width, rows = x.shape
    w_up, times = others[3], others[-1]
    size = w_up.shape[0]
    slots, cond = times.shape
    buffers, semaphores = scratch_plan(n_wide, rows, width, size, cond)
    anywhere = pl.BlockSpec(memory_space=pl.ANY)
    part, planes, groups = rows // 4, n_wide // 2, n_wide // 8
    outs = (
        ((width, rows), BF16),
        ((width, rows), F32),
        ((4, part, 128), BF16),
        ((4, part, 128), BF16),
        ((4, part // 2, 128), BF16),
        ((4, part // 2, 128), BF16),
        ((CHUNKS, size, size), BF16),
        ((2, planes, 4, MSG_ROWS, size), BF16),
        ((CHUNKS, groups, size // 4, size), BF16),
        ((cond, 6 * size), F32),
        ((6 * size,), F32),
        ((size,), F32),
        ((size,), F32),
        ((size,), F32),
        ((size,), F32),
        ((slots, cond), F32),
    )
    return pl.pallas_call(
        functools.partial(layer_kernel, n_wide, rows, width, size, cond, slots),
        out_shape=tuple(jax.ShapeDtypeStruct(shape, kind) for shape, kind in outs),
        in_specs=[pl.BlockSpec(memory_space=pltpu.SMEM)] + [anywhere] * (1 + len(others)),
        out_specs=(anywhere,) * len(outs),
        scratch_shapes=[pltpu.VMEM(shape, kind) for shape, kind in buffers.values()]
        + [pltpu.SemaphoreType.DMA(shape) for shape in semaphores.values()],
        compiler_params=pltpu.CompilerParams(
            collective_id=0, has_side_effects=True, vmem_limit_bytes=63 * 1024 * 1024
        ),
        name="layer",
    )(lengths, x, *others)


def body(
    n_wide,
    block_input,
    time_embed,
    seq_lengths,
    w_qkv,
    w_out,
    w_up,
    b_up,
    w_down,
    b_down,
    gain_one,
    gain_two,
    w_ada,
    b_ada,
    out_grad,
):
    size = w_up.shape[0]
    quarter = w_qkv.shape[2]
    out_t, in_t, _, _, _, _, g_own, _, _, ada, b_ada_sum, b_down_sum, gain_one_sum, gain_two_sum, b_up_sum, times = layer(
        n_wide, seq_lengths, block_input.T, out_grad.T, jnp.swapaxes(w_qkv, 1, 2), w_out, w_up, w_down, b_up,
        b_down, gain_one, gain_two, w_ada, b_ada, time_embed,
    )
    g_attn = g_own[0].astype(F32)
    grad_qkv = jnp.swapaxes(g_attn[: 3 * quarter].reshape(3, quarter, size), 1, 2)
    return (
        out_t.T,
        in_t.T,
        times,
        grad_qkv,
        g_attn[3 * quarter :],
        g_own[1].astype(F32),
        b_up_sum,
        g_own[2].astype(F32),
        b_down_sum,
        gain_one_sum,
        gain_two_sum,
        ada,
        b_ada_sum,
    )


def solution(mesh):
    return jax.shard_map(
        functools.partial(body, mesh.shape["wide"]),
        mesh=mesh,
        in_specs=(
            P("wide", "narrow"),
            P("wide", None),
            P("wide", None),
            P(None, None, "narrow"),
            P("narrow", None),
            P(None, "narrow"),
            P("narrow"),
            P("narrow", None),
            P(),
            P(),
            P(),
            P(),
            P(),
            P("wide", "narrow"),
        ),
        out_specs=(
            P("wide", "narrow"),
            P("wide", "narrow"),
            P("wide", None),
            P(None, None, "narrow"),
            P("narrow", None),
            P(None, "narrow"),
            P("narrow"),
            P("narrow", None),
            P(),
            P(),
            P(),
            P(),
            P(),
        ),
        check_vma=False,
    )
```

time: 804 us -> 192 us (0.24)
  waiting for transfers between devices: 498 us -> 0 us
  Pallas kernels: 0 us -> 175 us
  matrix products: 158 us -> 0 us
  other arithmetic: 63.7 us -> 4.62 us
  blocking collectives: 28.1 us -> 0 us
  local copies, waits for them, and re-layouts: 28.8 us -> 9 us
  between operations: 15.3 us -> 0.7 us
    psum x4 -> x0, waiting for transfers between devices: 421 us -> none  [the longest x1 155 us: body(): lax.psum(feed_partial.astype(jnp.bfloat16), 'narrow').astype(jnp.float32)]
    pallas_call x0 -> x1, Pallas kernels: none -> 175 us  [layer(): pl.pallas_call(functools.partial(layer_kernel, n_wide, rows, width, size,...]
    dot_general x47 -> x0, matrix products: 156 us -> none  [the longest x6 30.2 us: body(): jnp.dot(slot_table, modulation[:, piece_index * model_width:(piece_index...]
    all_gather x2 -> x0, waiting for transfers between devices: 75.9 us -> none  [the longest x1 46.6 us: body(): lax.all_gather(block_input, 'narrow', axis=1, tiled=True)]
    psum x1 -> x0, blocking collectives: 28.1 us -> none  [body(): lax.psum((grad_qkv, grad_out, grad_up, grad_bias_up, grad_down, grad_bias...]
    reduce_sum x11 -> x0, other arithmetic: 27.6 us -> none  [the longest x3 7.78 us: attend(): row_total = jnp.sum(expos, axis=-1, keepdims=True)]
    convert_element_type x6 -> x1, other arithmetic: 18.4 us -> 4.62 us  [body(): g_own[2].astype(F32)]
    unnamed x128 -> x27, local copies, waits for them, and re-layouts: 18.1 us -> 6.83 us
  transfers between devices with their start and end apart: 6 -> 0, of which waited for: 6 -> 0; matrix products, arithmetic and copies ran while one was open for 9% -> 0% of each run, Pallas kernels for 0% -> 0%
where the time goes in v2:
time: 192 us; the launch traced here: 190 us
  Pallas kernels  175 us (91%)
  local copies, waits for them, and re-layouts  9 us (5%)
  other arithmetic  4.62 us (2%)
    pallas_call x1, Pallas kernels, layer(): pl.pallas_call(functools.partial(layer_kernel, n_wide, rows, width, size,...  175 us
    unnamed x27, local copies, waits for them, and re-layouts  6.83 us
    convert_element_type x1, other arithmetic, body(): g_own[2].astype(F32)  4.62 us

profile of v2, /device:TPU:0, one launch (start us, length us, event | category | flops | bytes accessed | tf_op | source)
XLA Modules:
  0.0 189.8 jit_solution(11537948976122874386)
XLA Ops:
  0.7 175.4 %layer.1 = (bf16[192,1536]{1,0:T(8,128)(2,1)}, f32[192,1536]{1,0:T(8,128)}, bf16[4,384,128]{2,1,0:T(8,128)(2,1)}, bf16[4,384,128]{2,1,0:T(8,128)(2,1)}, bf16[4,1...) custom-call(s32[1,3]{1,0:T(1,128)} %refs_0_.1, ...), custom_call_target="tpu_custom_call" | custom-call | tf_op jit(solution)/shard_map/layer/pallas_call | solution.py:1309
  176.1 4.6 %bitcast_convert_fusion = (f32[768,768]{1,0:T(8,128)}, f32[768,768]{1,0:T(8,128)}, f32[1,768,768]{2,1,0:T(8,128)S(1)}) fusion(bf16[3,768,768]{2,1,0:T(8,128)(2,1)} %get-tuple-element.26), kind=kLoop, calls=%fused_computation | loop fusion | flops 1769472 | bytes 10616832 | tf_op jit(solution)/shard_map/convert_element_type | solution.py:1356
  180.7 0.9 slice_bitcast_fusion
  181.6 1.3 slice.25
  182.9 0.0 copy-start.4
  182.9 0.0 copy-start
  182.9 0.0 copy-done.2
  182.9 0.8 copy.36
  183.7 0.0 copy-done.1
  183.7 1.0 copy.37
  184.8 0.0 copy-done.8
  184.8 0.6 copy.38
  185.3 0.0 copy-done.7
  185.3 0.6 copy.39
  185.9 0.0 copy-done.6
  185.9 0.6 copy.40
  186.5 0.0 copy-done.5
  186.5 0.6 copy.41
  187.1 0.0 copy-done.4
  187.1 0.6 copy.42
  187.7 0.0 copy-done
  187.7 1.4 copy.43
  189.1 0.0 copy-done.3
  189.1 0.6 copy.44
  (7 shorter events, 0.0 us)
Async XLA Ops:
  180.7 2.2 %copy-start.2 = (bf16[192,1536]{1,0:T(8,128)(2,1)S(1)}, bf16[192,1536]{1,0:T(8,128)(2,1)}, u32[]{:S(2)}) copy-start(bf16[192,1536]{1,0:T(8,128)(2,1)} %get-tuple-element.23) | copy-start | bytes 1769476
  181.6 2.2 %copy-start.1 = (f32[192,1536]{1,0:T(8,128)S(1)}, f32[192,1536]{1,0:T(8,128)}, u32[]{:S(2)}) copy-start(f32[192,1536]{1,0:T(8,128)} %get-tuple-element.24) | copy-start | bytes 3538948
  182.9 1.9 copy-start.8
  182.9 2.5 %copy-start.7 = (f32[768]{0:T(1024)S(1)}, f32[768]{0:T(1024)}, u32[]{:S(2)}) copy-start(f32[768]{0:T(1024)} %get-tuple-element.55) | copy-start | bytes 9220
  182.9 3.1 %copy-start.6 = (f32[768]{0:T(1024)S(1)}, f32[768]{0:T(1024)}, u32[]{:S(2)}) copy-start(f32[768]{0:T(1024)} %get-tuple-element.57) | copy-start | bytes 9220
  182.9 3.6 %copy-start.5 = (f32[768]{0:T(1024)S(1)}, f32[768]{0:T(1024)}, u32[]{:S(2)}) copy-start(f32[768]{0:T(1024)} %get-tuple-element.58) | copy-start | bytes 9220
  182.9 4.2 %copy-start.4 = (f32[768]{0:T(1024)S(1)}, f32[768]{0:T(1024)}, u32[]{:S(2)}) copy-start(f32[768]{0:T(1024)} %get-tuple-element.59) | copy-start | bytes 9220
  182.9 4.8 %copy-start = (f32[128,4608]{1,0:T(8,128)S(1)}, f32[128,4608]{1,0:T(8,128)}, u32[]{:S(2)}) copy-start(f32[128,4608]{1,0:T(8,128)} %get-tuple-element.60) | copy-start | bytes 7077892
  187.7 1.4 copy-start.3

commit v3 on v2

--- a/solution.py
+++ b/solution.py
@@ -48,6 +48,8 @@
 
 
 TILE = 256
+ATTEND = 384
+ATTEND_BACK = 384
 
 
 def tiles(count, step, size=TILE):
@@ -125,7 +127,7 @@
     rows = q.shape[0]
 
     def step(s, start):
-        first = first_rows(bound, start, TILE)
+        first = first_rows(bound, start, ATTEND)
         column = lax.broadcasted_iota(jnp.int32, (1, rows), 1).astype(F32) < bound
         bias = jnp.where(first == column, 0.0, -1e30)
         halves = []
@@ -141,7 +143,7 @@
         lane = lax.broadcasted_iota(jnp.int32, halves[0].shape, 1)
         mixed[s, lanes(g)] = jnp.where(lane < HD, halves[0], halves[1]).astype(BF16)
 
-    tiles(rows, step)
+    tiles(rows, step, ATTEND)
 
 
 def mix_out(mixed, w_attn, part, share):
@@ -208,28 +210,30 @@
     tiles(dy.shape[0], step)
 
 
-def feed_back(feed_low, slope, w_up, w_down, bias_up, part, share):
+def feed_back(feed_low, slope, w_down, bias_up):
     def step(s, start):
         low = feed_low[s, :]
-        total = None
         for n in range(2):
             grad_pre = nt(low, w_down[n]) * slope[n, s, :].astype(F32)
             bias_up[n : n + 1, :] += jnp.sum(grad_pre, axis=0, keepdims=True)
-            pre = grad_pre.astype(BF16)
-            slope[n, s, :] = pre
-            term = nt(pre, w_up[n])
-            total = term if total is None else total + term
-        part[0, s, :] = total.astype(BF16)
+            slope[n, s, :] = grad_pre.astype(BF16)
+
+    tiles(feed_low.shape[0], step)
+
+
+def feed_in_back(pre_low, w_up, part, share):
+    def step(s, start):
+        part[0, s, :] = (nt(pre_low[0, s, :], w_up[0]) + nt(pre_low[1, s, :], w_up[1])).astype(BF16)
         share(s, start)
 
-    tiles(feed_low.shape[0], step)
+    tiles(pre_low.shape[1], step)
 
 
 def weight_grad(left, right, target):
     def step(s, start):
         target[s, :] = tn(left[:, s], right[...]).astype(BF16)
 
-    size = TILE if left.shape[1] % TILE == 0 else 128
+    size = 384 if left.shape[1] % 384 == 0 else 128
     tiles(left.shape[1], step, size)
 
 
@@ -280,7 +284,7 @@
         pair = jnp.where(lane < HD, halves[0], halves[1]) * 0.125
         grad_q[s, lanes(g)] = turned_back(pair, s).astype(BF16)
 
-    tiles(rows, step)
+    tiles(rows, step, ATTEND_BACK)
 
     def finish(s, start):
         grad_k[s, lanes(g)] = turned_back(total_k[s, :] * (1.0 / LOG2_E), s).astype(BF16)
@@ -315,13 +319,13 @@
 ROW_B_UP, ROW_B_DOWN, ROW_GAIN_ONE, ROW_GAIN_TWO, ROW_B_ADA = 0, 1, 2, 3, 8
 MSG_MOD, MSG_B_DOWN, MSG_GAIN_ONE, MSG_GAIN_TWO, MSG_B_UP, MSG_CONTEXT = 0, 6, 7, 8, 9, 11
 MSG_ROWS = 16
+Z_SLOT = (0, 3, 5)
 
 
 def scratch_plan(n_wide, rows, width, size, cond):
     half, heads = rows // 2, 2 * width // HD
     block = size // 4
     buffers = {
-        "raw": ((2, width, rows), BF16),
         "tail": ((half // 2, 128), F32),
         "small": ((16, size), F32),
         "b_all": ((4, 8, size), F32),
@@ -366,12 +370,12 @@
         "g_ff": ((2, 2, size, size), BF16),
         "near_half": ((CHUNKS, 2, 2, block // 2, size), BF16),
         "near_full": ((CHUNKS, 2, 2, block, size), BF16),
-        "from_z": ((CHUNKS, 3, block, size), BF16),
+        "from_z": ((7, block, size), BF16),
     }
     planes = n_wide // 2
     groups = n_wide // 8
     semaphores = {
-        "load": (26,),
+        "load": (28,),
         "msg_load": (n_wide, 4),
         "end_small": (17,),
         "pair": (4,),
@@ -410,7 +414,7 @@
     buffers, semaphores = scratch_plan(n_wide, rows, width, size, cond)
     names = (
         ["lengths", "x", "dy", "w_qkv", "w_out", "w_up", "w_down", "b_up", "b_down", "gain_one", "gain_two", "w_ada"]
-        + ["b_ada", "times", "out_t", "in_t", "out_o", "in_o", "out_r", "in_r", "g_out", "messages", "groups"]
+        + ["b_ada", "times", "out_t", "in_t", "out_o", "in_o", "out_r", "in_r", "g_heads", "g_up", "g_down", "messages", "groups"]
         + ["ada_out", "b_ada_out", "b_down_out", "gain_one_out", "gain_two_out", "b_up_out", "time_out"]
         + list(buffers)
     )
@@ -439,8 +443,11 @@
         pl.semaphore_signal(barrier, inc=1, device_id=device, device_id_type=MESH)
 
     w_ada = r.probs.at[2]
-    loads = [pltpu.make_async_copy(r.x, r.raw.at[0], sem.load.at[0])]
-    loads.append(pltpu.make_async_copy(r.dy, r.raw.at[1], sem.load.at[1]))
+    raw = r.probs.at[3]
+    loads = []
+    for i in range(4):
+        source = (r.x, r.dy)[i // 2].at[:, pl.ds((i % 2) * half, half)]
+        loads.append(pltpu.make_async_copy(source, raw.at[pl.ds(i * width, width)], sem.load.at[(0, 1, 26, 27)[i]]))
     for i, ref in enumerate((r.b_up, r.b_down, r.gain_one, r.gain_two)):
         loads.append(pltpu.make_async_copy(ref, r.small.at[i], sem.load.at[2 + i]))
     for i in range(6):
@@ -519,10 +526,10 @@
                 for copy in home_copies(t, q):
                     copy.start()
 
-    def weights_own(t):
+    def weights_own(t, at_edge):
         for q in range(2):
 
-            @pl.when(far[q] != 0)
+            @pl.when((z == edge) if at_edge else (far[q] != 0) & (z != edge))
             def _():
                 landed(w_block(t, q, mine), sem.z_in.at[t, q])
 
@@ -612,11 +619,16 @@
 
     def turn_rows(kind):
         back = jnp.where(shift == 0, 0, rows - shift)
-        r.raw[kind] = pltpu.roll(r.raw[kind].astype(F32), back, 1).astype(BF16)
+        at = 2 * kind * width
+        columns = jnp.concatenate([raw[at : at + width, :], raw[at + width : at + 2 * width, :]], axis=1)
+        columns = pltpu.roll(columns.astype(F32), back, 1).astype(BF16)
+        raw[at : at + width, :] = columns[:, :half]
+        raw[at + width : at + 2 * width, :] = columns[:, half:]
         same = unit(part)
         r.tail[...] = jnp.zeros_like(r.tail)
         for j in range(4):
-            turned = nt(same, r.raw[kind, :, j * part : (j + 1) * part])
+            row, lane_at = at + (j // 2) * width, (j % 2) * part
+            turned = nt(same, raw[row : row + width, lane_at : lane_at + part])
             main = turned[:, :128]
             r.tail[:, : width - 128] = turned[:, 128:]
             tail = r.tail[...]
@@ -720,11 +732,11 @@
 
     def g_home(t, q, slot):
         return remote(
-            g_block(t, q, mine), r.from_z.at[t, slot], sem.g_send.at[t, q, 4], sem.gz_in.at[t, slot], (w, 2 * c + q)
+            g_block(t, q, mine), r.from_z.at[Z_SLOT[t] + slot], sem.g_send.at[t, q, 4], sem.gz_in.at[t, slot], (w, 2 * c + q)
         )
 
     def g_edge(t, q):
-        return remote(g_block(t, q, mine), r.from_z.at[t, q], sem.g_send.at[t, q, 4], sem.gz_in.at[t, q], (w, middle))
+        return remote(g_block(t, q, mine), r.from_z.at[Z_SLOT[t] + q], sem.g_send.at[t, q, 4], sem.gz_in.at[t, q], (w, middle))
 
     def grads_start(t, q):
         g_copy(t, q, 0).start()
@@ -764,12 +776,14 @@
         @pl.when(z == middle)
         def _():
             for q in range(2):
-                landed(r.from_z.at[t, q], sem.gz_in.at[t, q])
-                add_to(g_block(t, q, mine), [r.from_z.at[t, q]])
+                landed(r.from_z.at[Z_SLOT[t] + q], sem.gz_in.at[t, q])
+                add_to(g_block(t, q, mine), [r.from_z.at[Z_SLOT[t] + q]])
                 g_home(t, q, 1).start()
 
     def out_block(t, index, start=0, count=block):
-        return r.g_out.at[t, pl.ds(pl.multiple_of(index * block + start, 32), count)]
+        if t == 0:
+            return r.g_heads.at[index, pl.ds(start, count)]
+        return (r.g_up, r.g_down)[t - 1].at[pl.ds(pl.multiple_of(index * block + start, 32), count)]
 
     def end_local(t, q):
         return pltpu.make_async_copy(g_block(t, q, mine), out_block(t, mine), sem.end_in.at[t, 4])
@@ -780,6 +794,11 @@
                 g_block(t, q, mine), out_block(t, mine), sem.end_send.at[t, n], sem.end_in.at[t, n],
                 (next_x, next_y)[n],
             )
+        if t == 0:
+            return remote(
+                g_block(t, q, mine), out_block(t, mine), sem.end_send.at[t, 2], sem.end_in.at[t, 2],
+                (flip(next_x[0], by, 4), z),
+            )
         ref = out_block(t, block_x, 0, block // 2) if n == 2 else out_block(t, block_y, block // 2, block // 2)
         return remote(ref, ref, sem.end_send.at[t, n], sem.end_in.at[t, n], (next_y, next_x)[n - 2])
 
@@ -800,20 +819,22 @@
             def _():
                 count = 3 if t == 0 else 2
                 for slot in range(count):
-                    landed(r.from_z.at[t, slot], sem.gz_in.at[t, slot])
-                add_to(g_block(t, q, mine), [r.from_z.at[t, slot] for slot in range(count)])
+                    landed(r.from_z.at[Z_SLOT[t] + slot], sem.gz_in.at[t, slot])
+                add_to(g_block(t, q, mine), [r.from_z.at[Z_SLOT[t] + slot] for slot in range(count)])
                 for step in range(1, groups):
                     group_copy(t, q, step).start()
                 for step in range(1, groups):
                     group_copy(t, q, step).wait()
                 for step in range(1, groups):
-                    load = pltpu.make_async_copy(r.groups.at[t, step], r.from_z.at[t, 0], sem.group_load.at[t])
+                    load = pltpu.make_async_copy(r.groups.at[t, step], r.from_z.at[Z_SLOT[t]], sem.group_load.at[t])
                     load.start()
                     load.wait()
-                    add_to(g_block(t, q, mine), [r.from_z.at[t, 0]])
+                    add_to(g_block(t, q, mine), [r.from_z.at[Z_SLOT[t]]])
                 end_local(t, q).start()
                 end_copy(t, q, 0).start()
                 end_copy(t, q, 1).start()
+                if t == 0:
+                    end_copy(t, q, 2).start()
 
     def grads_fifth(t):
         for q in range(2):
@@ -821,10 +842,12 @@
             @pl.when(far[q] == 0)
             def _():
                 landed(out_block(t, block_x), sem.end_in.at[t, 0])
-                end_copy(t, q, 2).start()
+                if t > 0:
+                    end_copy(t, q, 2).start()
                 end_pair(t, 1).start()
                 landed(out_block(t, block_y), sem.end_in.at[t, 1])
-                end_copy(t, q, 3).start()
+                if t > 0:
+                    end_copy(t, q, 3).start()
                 end_pair(t, 2).start()
                 end_local(t, q).wait()
                 end_pair(t, 0).start()
@@ -834,8 +857,11 @@
 
             @pl.when(far[q] == 0)
             def _():
-                landed(out_block(t, block_d, 0, block // 2), sem.end_in.at[t, 2])
-                landed(out_block(t, block_d, block // 2, block // 2), sem.end_in.at[t, 3])
+                if t == 0:
+                    landed(out_block(t, block_d), sem.end_in.at[t, 2])
+                else:
+                    landed(out_block(t, block_d, 0, block // 2), sem.end_in.at[t, 2])
+                    landed(out_block(t, block_d, block // 2, block // 2), sem.end_in.at[t, 3])
                 end_pair(t, 3).start()
 
     def grads_done(t):
@@ -849,7 +875,7 @@
 
             @pl.when(far[q] == 0)
             def _():
-                for n in range(4):
+                for n in range(3 if t == 0 else 4):
                     end_copy(t, q, n).wait_send()
                 for n in range(4):
                     end_pair(t, n).wait_send()
@@ -1018,17 +1044,17 @@
         times = r.info[0]
         gate = 1.0 / (1.0 + jnp.exp(-times))
         r.context[...] = grads * (gate + times * gate * (1.0 - gate))
-        copies = [
-            pltpu.make_async_copy(r.grad_one.at[pl.ds(i * cond, cond)], r.ada_out.at[:, pl.ds(i * size, size)], sem.end_small.at[i])
-            for i in range(6)
-        ]
-        copies += [
-            pltpu.make_async_copy(r.small.at[i], r.b_ada_out.at[pl.ds(i * size, size)], sem.end_small.at[6 + i])
-            for i in range(6)
-        ]
-        for i, (row, ref) in enumerate(
-            ((MSG_B_DOWN, r.b_down_out), (MSG_GAIN_ONE, r.gain_one_out), (MSG_GAIN_TWO, r.gain_two_out), (MSG_B_UP, r.b_up_out))
-        ):
+        copies = []
+        for i in range(6):
+            ends = (r.grad_one.at[pl.ds(i * cond, cond)], r.ada_out.at[:, pl.ds(i * size, size)])
+            copies.append(pltpu.make_async_copy(*ends, sem.end_small.at[i]))
+            ends = (r.small.at[i], r.b_ada_out.at[pl.ds(i * size, size)])
+            copies.append(pltpu.make_async_copy(*ends, sem.end_small.at[6 + i]))
+        rows_out = (
+            (MSG_B_DOWN, r.b_down_out), (MSG_GAIN_ONE, r.gain_one_out), (MSG_GAIN_TWO, r.gain_two_out),
+            (MSG_B_UP, r.b_up_out),
+        )
+        for i, (row, ref) in enumerate(rows_out):
             copies.append(pltpu.make_async_copy(r.small.at[row], ref, sem.end_small.at[12 + i]))
         copies.append(pltpu.make_async_copy(r.context.at[pl.ds(0, slots)], r.time_out, sem.end_small.at[16]))
         for copy in copies:
@@ -1041,7 +1067,7 @@
     for i in range(slots):
         length_row = jnp.where(lane == i, r.lengths[0, i].astype(F32), length_row)
     r.info[0, slots : slots + 1, :] = length_row
-    for load in loads[2:6]:
+    for load in loads[4:8]:
         load.wait()
     r.b_own[...] = r.small[0:8, :]
 
@@ -1054,9 +1080,6 @@
     ]
     for copy in b_copies:
         copy.start()
-    loads[0].wait()
-    turn_rows(0)
-    rows_start(0)
 
     info_copy.wait()
     info = jnp.where(home, r.info[0], r.info[1])
@@ -1084,7 +1107,7 @@
     bound = jnp.where(odd, pick(slot_after(1), spans), float(half))
     r.context[0:1, :] = pick(flags_a, [context[i : i + 1, :] for i in range(slots)])
     r.context[1:2, :] = pick(flags_b, [context[i : i + 1, :] for i in range(slots)])
-    for load in loads[6:]:
+    for load in loads[8:]:
         load.wait()
     rises = {}
     for i in range(6):
@@ -1111,15 +1134,21 @@
     r.scales[...] = jnp.zeros_like(r.scales)
     r.sums[...] = jnp.zeros_like(r.sums)
     r.bias_up[...] = jnp.zeros_like(r.bias_up)
-    weights_own(0)
+    loads[0].wait()
     loads[1].wait()
+    turn_rows(0)
+    rows_start(0)
+    weights_own(0, False)
+    loads[2].wait()
+    loads[3].wait()
     turn_rows(1)
+    weights_own(0, True)
     for n, copy in enumerate(b_copies):
         landed(r.b_all.at[(z + 3 - n) % 4], sem.b_in.at[n + 1])
     r.b_all[z] = r.b_own[...]
     weights_pass(0)
+    rows_join(0)
     weights_start(1)
-    rows_join(0)
     weights_done(0)
 
     def project_some(i, carry):
@@ -1135,14 +1164,16 @@
 
     lax.fori_loop(0, 4, project_some, 0)
     weights_start(2)
-    weights_own(1)
+    weights_own(1, False)
     rows_sent(0)
     attend(bound, 0, r.q, r.k, r.v, r.probs, r.scales, r.mixed)
-    weights_pass(1)
+    weights_own(1, True)
     rows_start(1)
     attend(bound, 1, r.q, r.k, r.v, r.probs, r.scales, r.mixed)
-    weights_own(2)
+    weights_pass(1)
+    weights_own(2, False)
     attend(bound, 2, r.q, r.k, r.v, r.probs, r.scales, r.mixed)
+    weights_own(2, True)
     mix_out(r.mixed, r.w_attn, r.attn_part, sharing(0, r.attn_part))
     weights_done(1)
     b_up = jnp.where(c == 0, r.b_all[0, 0:1, :], r.b_all[2, 0:1, :]), jnp.where(c == 0, r.b_all[1, 0:1, :], r.b_all[3, 0:1, :])
@@ -1160,13 +1191,12 @@
     weights_done(2)
     feed_down(r.act, r.w_ff.at[1], r.feed_part, sharing(1, r.feed_part))
     grads_second(2, 0)
-    feed_back(
-        r.feed_low, r.slope, r.w_ff.at[0], r.w_ff.at[1], r.bias_up, r.back_part, sharing(2, r.back_part)
-    )
+    feed_back(r.feed_low, r.slope, r.w_ff.at[1], r.bias_up)
     grads_second(2, 1)
     for q in range(2):
         weight_grad(r.in_two, r.slope.at[q], r.g_ff.at[0, q])
         grads_start(1, q)
+    feed_in_back(r.slope, r.w_ff.at[0], r.back_part, sharing(2, r.back_part))
     b_down = r.small[ROW_B_DOWN : ROW_B_DOWN + 1, :]
     feed_out(
         bound, r.x_low, r.dy_low, r.mods, r.attn_part, r.feed_part, b_down, r.out_low, r.sums, arriving(1, r.feed_part)
@@ -1235,13 +1265,13 @@
         copy.start()
     for load in ada_loads:
         load.start()
-    results_start(1, r.in_two)
     results_done(0, r.out_low)
     results_turn(0, r.act.at[0], r.out_t, r.feed_low)
     grads_middle(1)
     grads_third(0)
     grads_fourth(2)
     grads_fourth(1)
+    results_start(1, r.in_two)
     message_local.wait()
     for dz in range(1, 4):
         landed(r.messages.at[c, plane_at, (z + 4 - dz) % 4], sem.m_in.at[dz])
@@ -1253,22 +1283,22 @@
         )
         plane_copies[-1].start()
     grads_fifth(2)
-    results_done(1, r.in_two)
-    results_turn(1, r.act.at[1], r.in_t, r.grad_one)
+    grads_fifth(1)
     for step in range(1, planes):
         landed(r.messages.at[c, (plane_at + planes - step) % planes], sem.mp_in.at[step])
     message_pair = remote(r.messages.at[c], r.messages.at[c], sem.m_send.at[4], sem.m_in.at[4], pair)
     message_pair.start()
     grads_fourth(0)
-    grads_fifth(1)
     grads_sixth(2)
+    grads_sixth(1)
     landed(r.messages.at[1 - c], sem.m_in.at[4])
     small_ends = finish_small()
     grads_fifth(0)
-    grads_sixth(1)
-    grads_sixth(0)
     for copy in small_ends:
         copy.wait()
+    results_done(1, r.in_two)
+    results_turn(1, r.act.at[1], r.in_t, r.grad_one)
+    grads_sixth(0)
 
     for t in range(CHUNKS):
         weights_sent(t)
@@ -1295,7 +1325,9 @@
         ((4, part, 128), BF16),
         ((4, part // 2, 128), BF16),
         ((4, part // 2, 128), BF16),
-        ((CHUNKS, size, size), BF16),
+        ((4, size // 4, size), BF16),
+        ((size, size), BF16),
+        ((size, size), BF16),
         ((2, planes, 4, MSG_ROWS, size), BF16),
         ((CHUNKS, groups, size // 4, size), BF16),
         ((cond, 6 * size), F32),
@@ -1337,23 +1369,21 @@
     b_ada,
     out_grad,
 ):
-    size = w_up.shape[0]
-    quarter = w_qkv.shape[2]
-    out_t, in_t, _, _, _, _, g_own, _, _, ada, b_ada_sum, b_down_sum, gain_one_sum, gain_two_sum, b_up_sum, times = layer(
+    results = layer(
         n_wide, seq_lengths, block_input.T, out_grad.T, jnp.swapaxes(w_qkv, 1, 2), w_out, w_up, w_down, b_up,
         b_down, gain_one, gain_two, w_ada, b_ada, time_embed,
     )
-    g_attn = g_own[0].astype(F32)
-    grad_qkv = jnp.swapaxes(g_attn[: 3 * quarter].reshape(3, quarter, size), 1, 2)
+    out_t, in_t, _, _, _, _, g_heads, g_up, g_down, _, _ = results[:11]
+    ada, b_ada_sum, b_down_sum, gain_one_sum, gain_two_sum, b_up_sum, times = results[11:18]
     return (
         out_t.T,
         in_t.T,
         times,
-        grad_qkv,
-        g_attn[3 * quarter :],
-        g_own[1].astype(F32),
+        jnp.swapaxes(g_heads[:3].astype(F32), 1, 2),
+        g_heads[3].astype(F32),
+        g_up.astype(F32),
         b_up_sum,
-        g_own[2].astype(F32),
+        g_down.astype(F32),
         b_down_sum,
         gain_one_sum,
         gain_two_sum,

time: 192 us -> 193 us (level)
  other arithmetic: 4.62 us -> 7.58 us
    transpose x0 -> x1, other arithmetic: none -> 2.61 us  [body(): jnp.swapaxes(g_heads[:3].astype(F32), 1, 2)]
    slice x2 -> x0, local copies, waits for them, and re-layouts: 2.17 us -> none  [the longest x1 1.32 us: body(): g_attn[:3 * quarter].reshape(3, quarter, size)]
    unnamed x27 -> x31, local copies, waits for them, and re-layouts: 6.83 us -> 7.59 us
    convert_element_type x1 -> x3, other arithmetic: 4.62 us -> 4.97 us  [the longest x1 1.82 us: body(): g_heads[3].astype(F32)]
where the time goes in v3:
time: 193 us; the launch traced here: 191 us
  Pallas kernels  175 us (91%)
  local copies, waits for them, and re-layouts  7.59 us (4%)
  other arithmetic  7.58 us (4%)
    pallas_call x1, Pallas kernels, layer(): pl.pallas_call(functools.partial(layer_kernel, n_wide, rows, width, size,...  175 us
    unnamed x31, local copies, waits for them, and re-layouts  7.59 us

profile of v3, /device:TPU:0, one launch (start us, length us, event | category | flops | bytes accessed | tf_op | source)
XLA Modules:
  0.0 191.1 jit_solution(8405110706399319052)
XLA Ops:
  0.7 175.2 %layer.1 = (bf16[192,1536]{1,0:T(8,128)(2,1)}, f32[192,1536]{1,0:T(8,128)}, bf16[4,384,128]{2,1,0:T(8,128)(2,1)}, bf16[4,384,128]{2,1,0:T(8,128)(2,1)}, bf16[4,1...) custom-call(s32[1,3]{1,0:T(1,128)} %refs_0_.1, ...), custom_call_target="tpu_custom_call" | custom-call | tf_op jit(solution)/shard_map/layer/pallas_call | solution.py:1341
  175.9 1.8 bitcast_convert_fusion
  177.7 2.6 %convert_bitcast_fusion = f32[3,768,192]{1,2,0:T(8,128)} fusion(bf16[4,192,768]{2,1,0:T(8,128)(2,1)} %get-tuple-element.28), kind=kLoop, calls=%fused_computation | loop fusion | flops 442368 | bytes 2654208 | tf_op jit(solution)/shard_map/transpose | solution.py:1382
  180.3 0.0 copy-done.2
  180.3 1.6 convert_element_type.15
  181.9 0.1 copy-done.1
  182.0 1.6 convert_element_type.16
  183.6 0.0 copy-done.4
  183.6 0.8 copy.36
  184.4 0.7 copy-done.3
  185.1 1.0 copy.37
  186.1 0.0 copy-done.10
  186.1 0.6 copy.38
  186.7 0.0 copy-done.9
  186.7 0.6 copy.39
  187.3 0.0 copy-done.8
  187.3 0.6 copy.40
  187.9 0.0 copy-done.7
  187.9 0.6 copy.41
  188.5 0.0 copy-done.6
  188.5 0.6 copy.42
  189.1 0.0 copy-done
  189.1 1.4 copy.43
  190.5 0.6 copy.44
  (12 shorter events, 0.0 us)
Async XLA Ops:
  177.7 2.6 %copy-start.2 = (bf16[768,768]{1,0:T(8,128)(2,1)S(1)}, bf16[768,768]{1,0:T(8,128)(2,1)}, u32[]{:S(2)}) copy-start(bf16[768,768]{1,0:T(8,128)(2,1)} %get-tuple-element.29) | copy-start | bytes 3538948
  180.3 1.7 copy-start.1
  182.0 1.6 copy-start.4
  182.0 4.1 %copy-start.10 = (f32[3,128]{1,0:T(4,128)S(1)}, f32[3,128]{1,0:T(4,128)}, u32[]{:S(2)}) copy-start(f32[3,128]{1,0:T(4,128)} %get-tuple-element.52) | copy-start | bytes 4612
  182.0 4.7 %copy-start.9 = (f32[768]{0:T(1024)S(1)}, f32[768]{0:T(1024)}, u32[]{:S(2)}) copy-start(f32[768]{0:T(1024)} %get-tuple-element.56) | copy-start | bytes 9220
  183.6 1.5 copy-start.3
  185.1 2.2 %copy-start.8 = (f32[768]{0:T(1024)S(1)}, f32[768]{0:T(1024)}, u32[]{:S(2)}) copy-start(f32[768]{0:T(1024)} %get-tuple-element.58) | copy-start | bytes 9220
  185.1 2.8 %copy-start.7 = (f32[768]{0:T(1024)S(1)}, f32[768]{0:T(1024)}, u32[]{:S(2)}) copy-start(f32[768]{0:T(1024)} %get-tuple-element.59) | copy-start | bytes 9220
  185.1 3.4 %copy-start.6 = (f32[768]{0:T(1024)S(1)}, f32[768]{0:T(1024)}, u32[]{:S(2)}) copy-start(f32[768]{0:T(1024)} %get-tuple-element.60) | copy-start | bytes 9220
  185.1 4.0 %copy-start = (f32[128,4608]{1,0:T(8,128)S(1)}, f32[128,4608]{1,0:T(8,128)}, u32[]{:S(2)}) copy-start(f32[128,4608]{1,0:T(8,128)} %get-tuple-element.61) | copy-start | bytes 7077892
  189.1 1.4 copy-start.5

commit v4 on v3

--- a/solution.py
+++ b/solution.py
@@ -641,16 +641,17 @@
             packed = left[: part // 2] + pltpu.roll(left[part // 2 :], 64, 1)
             stage[kind][j * (part // 2) : (j + 1) * (part // 2), rests : rests + 128] = packed.astype(BF16)
 
-    def rows_start(kind):
+    def rows_start(kind, outer):
         for j in range(4):
             own, here, there = row_copies(kind, j)
-
-            @pl.when(own)
+            wanted = (c == j // 2) == outer
+
+            @pl.when(wanted & own)
             def _():
                 for copy in here:
                     copy.start()
 
-            @pl.when(jnp.logical_not(own))
+            @pl.when(wanted & jnp.logical_not(own))
             def _():
                 for copy in there:
                     copy.start()
@@ -1137,8 +1138,9 @@
     loads[0].wait()
     loads[1].wait()
     turn_rows(0)
-    rows_start(0)
+    rows_start(0, True)
     weights_own(0, False)
+    rows_start(0, False)
     loads[2].wait()
     loads[3].wait()
     turn_rows(1)
@@ -1168,7 +1170,8 @@
     rows_sent(0)
     attend(bound, 0, r.q, r.k, r.v, r.probs, r.scales, r.mixed)
     weights_own(1, True)
-    rows_start(1)
+    rows_start(1, True)
+    rows_start(1, False)
     attend(bound, 1, r.q, r.k, r.v, r.probs, r.scales, r.mixed)
     weights_pass(1)
     weights_own(2, False)

time: 193 us -> 184 us (0.953)
  Pallas kernels: 175 us -> 166 us
    pallas_call x1, Pallas kernels: 175 us -> 166 us  [layer(): pl.pallas_call(functools.partial(layer_kernel, n_wide, rows, width, size,...]
where the time goes in v4:
time: 184 us; the launch traced here: 182 us
  Pallas kernels  166 us (90%)
  local copies, waits for them, and re-layouts  7.59 us (4%)
  other arithmetic  7.58 us (4%)
    pallas_call x1, Pallas kernels, layer(): pl.pallas_call(functools.partial(layer_kernel, n_wide, rows, width, size,...  166 us
    unnamed x31, local copies, waits for them, and re-layouts  7.59 us

profile of v4, /device:TPU:0, one launch (start us, length us, event | category | flops | bytes accessed | tf_op | source)
XLA Modules:
  0.0 181.9 jit_solution(8901251521418711460)
XLA Ops:
  0.7 166.0 %layer.1 = (bf16[192,1536]{1,0:T(8,128)(2,1)}, f32[192,1536]{1,0:T(8,128)}, bf16[4,384,128]{2,1,0:T(8,128)(2,1)}, bf16[4,384,128]{2,1,0:T(8,128)(2,1)}, bf16[4,1...) custom-call(s32[1,3]{1,0:T(1,128)} %refs_0_.1, ...), custom_call_target="tpu_custom_call" | custom-call | tf_op jit(solution)/shard_map/layer/pallas_call | solution.py:1344
  166.7 1.8 bitcast_convert_fusion
  168.5 2.6 %convert_bitcast_fusion = f32[3,768,192]{1,2,0:T(8,128)} fusion(bf16[4,192,768]{2,1,0:T(8,128)(2,1)} %get-tuple-element.28), kind=kLoop, calls=%fused_computation | loop fusion | flops 442368 | bytes 2654208 | tf_op jit(solution)/shard_map/transpose | solution.py:1385
  171.1 0.0 copy-done.2
  171.1 1.6 convert_element_type.15
  172.7 0.1 copy-done.1
  172.8 1.6 convert_element_type.16
  174.4 0.0 copy-done.4
  174.4 0.8 copy.36
  175.2 0.7 copy-done.3
  175.9 1.0 copy.37
  176.9 0.0 copy-done.10
  176.9 0.6 copy.38
  177.5 0.0 copy-done.9
  177.5 0.6 copy.39
  178.1 0.0 copy-done.8
  178.1 0.6 copy.40
  178.7 0.0 copy-done.7
  178.7 0.6 copy.41
  179.3 0.0 copy-done.6
  179.3 0.6 copy.42
  179.9 1.4 copy.43
  181.3 0.0 copy-done.5
  181.3 0.6 copy.44
  (12 shorter events, 0.0 us)
Async XLA Ops:
  168.5 2.6 %copy-start.2 = (bf16[768,768]{1,0:T(8,128)(2,1)S(1)}, bf16[768,768]{1,0:T(8,128)(2,1)}, u32[]{:S(2)}) copy-start(bf16[768,768]{1,0:T(8,128)(2,1)} %get-tuple-element.29) | copy-start | bytes 3538948
  171.1 1.7 copy-start.1
  172.8 1.6 copy-start.4
  172.8 4.1 %copy-start.10 = (f32[3,128]{1,0:T(4,128)S(1)}, f32[3,128]{1,0:T(4,128)}, u32[]{:S(2)}) copy-start(f32[3,128]{1,0:T(4,128)} %get-tuple-element.52) | copy-start | bytes 4612
  172.8 4.7 %copy-start.9 = (f32[768]{0:T(1024)S(1)}, f32[768]{0:T(1024)}, u32[]{:S(2)}) copy-start(f32[768]{0:T(1024)} %get-tuple-element.56) | copy-start | bytes 9220
  174.4 1.5 copy-start.3
  175.9 2.2 %copy-start.8 = (f32[768]{0:T(1024)S(1)}, f32[768]{0:T(1024)}, u32[]{:S(2)}) copy-start(f32[768]{0:T(1024)} %get-tuple-element.58) | copy-start | bytes 9220
  175.9 2.8 %copy-start.7 = (f32[768]{0:T(1024)S(1)}, f32[768]{0:T(1024)}, u32[]{:S(2)}) copy-start(f32[768]{0:T(1024)} %get-tuple-element.59) | copy-start | bytes 9220
  175.9 3.4 %copy-start.6 = (f32[768]{0:T(1024)S(1)}, f32[768]{0:T(1024)}, u32[]{:S(2)}) copy-start(f32[768]{0:T(1024)} %get-tuple-element.60) | copy-start | bytes 9220
  175.9 4.0 %copy-start = (f32[128,4608]{1,0:T(8,128)S(1)}, f32[128,4608]{1,0:T(8,128)}, u32[]{:S(2)}) copy-start(f32[128,4608]{1,0:T(8,128)} %get-tuple-element.61) | copy-start | bytes 7077892
  179.8 1.4 copy-start.5

commit v5 on v4

--- a/solution.py
+++ b/solution.py
@@ -414,7 +414,7 @@
     buffers, semaphores = scratch_plan(n_wide, rows, width, size, cond)
     names = (
         ["lengths", "x", "dy", "w_qkv", "w_out", "w_up", "w_down", "b_up", "b_down", "gain_one", "gain_two", "w_ada"]
-        + ["b_ada", "times", "out_t", "in_t", "out_o", "in_o", "out_r", "in_r", "g_heads", "g_up", "g_down", "messages", "groups"]
+        + ["b_ada", "times", "out_t", "in_t", "out_o", "in_o", "out_r", "in_r", "g_qkv", "g_o", "g_up", "g_down", "messages", "groups"]
         + ["ada_out", "b_ada_out", "b_down_out", "gain_one_out", "gain_two_out", "b_up_out", "time_out"]
         + list(buffers)
     )
@@ -783,8 +783,34 @@
 
     def out_block(t, index, start=0, count=block):
         if t == 0:
-            return r.g_heads.at[index, pl.ds(start, count)]
+            return r.g_o
         return (r.g_up, r.g_down)[t - 1].at[pl.ds(pl.multiple_of(index * block + start, 32), count)]
+
+    def heads_each(index, action):
+        @pl.when(index == 3)
+        def _():
+            action(r.g_o)
+
+        @pl.when(index != 3)
+        def _():
+            action(r.g_qkv.at[jnp.minimum(index, 2)])
+
+    def heads_leave(q):
+        def action(place):
+            pltpu.make_async_copy(g_block(0, q, mine), place, sem.end_in.at[0, 4]).start()
+            for n, device in enumerate((next_x, next_y, (flip(next_x[0], by, 4), z))):
+                remote(g_block(0, q, mine), place, sem.end_send.at[0, n], sem.end_in.at[0, n], device).start()
+
+        heads_each(mine, action)
+
+    def pair_start(t, n):
+        if t > 0:
+            end_pair(t, n).start()
+            return
+        heads_each(
+            (mine, block_x, block_y, block_d)[n],
+            lambda place: remote(place, place, sem.end_send.at[0, 4 + n], sem.end_in.at[0, 5 + n], pair).start(),
+        )
 
     def end_local(t, q):
         return pltpu.make_async_copy(g_block(t, q, mine), out_block(t, mine), sem.end_in.at[t, 4])
@@ -831,11 +857,12 @@
                     load.start()
                     load.wait()
                     add_to(g_block(t, q, mine), [r.from_z.at[Z_SLOT[t]]])
-                end_local(t, q).start()
-                end_copy(t, q, 0).start()
-                end_copy(t, q, 1).start()
                 if t == 0:
-                    end_copy(t, q, 2).start()
+                    heads_leave(q)
+                else:
+                    end_local(t, q).start()
+                    end_copy(t, q, 0).start()
+                    end_copy(t, q, 1).start()
 
     def grads_fifth(t):
         for q in range(2):
@@ -845,13 +872,13 @@
                 landed(out_block(t, block_x), sem.end_in.at[t, 0])
                 if t > 0:
                     end_copy(t, q, 2).start()
-                end_pair(t, 1).start()
+                pair_start(t, 1)
                 landed(out_block(t, block_y), sem.end_in.at[t, 1])
                 if t > 0:
                     end_copy(t, q, 3).start()
-                end_pair(t, 2).start()
+                pair_start(t, 2)
                 end_local(t, q).wait()
-                end_pair(t, 0).start()
+                pair_start(t, 0)
 
     def grads_sixth(t):
         for q in range(2):
@@ -863,7 +890,7 @@
                 else:
                     landed(out_block(t, block_d, 0, block // 2), sem.end_in.at[t, 2])
                     landed(out_block(t, block_d, block // 2, block // 2), sem.end_in.at[t, 3])
-                end_pair(t, 3).start()
+                pair_start(t, 3)
 
     def grads_done(t):
         for q in range(2):
@@ -1328,7 +1355,8 @@
         ((4, part, 128), BF16),
         ((4, part // 2, 128), BF16),
         ((4, part // 2, 128), BF16),
-        ((4, size // 4, size), BF16),
+        ((3, size // 4, size), BF16),
+        ((size // 4, size), BF16),
         ((size, size), BF16),
         ((size, size), BF16),
         ((2, planes, 4, MSG_ROWS, size), BF16),
@@ -1376,14 +1404,14 @@
         n_wide, seq_lengths, block_input.T, out_grad.T, jnp.swapaxes(w_qkv, 1, 2), w_out, w_up, w_down, b_up,
         b_down, gain_one, gain_two, w_ada, b_ada, time_embed,
     )
-    out_t, in_t, _, _, _, _, g_heads, g_up, g_down, _, _ = results[:11]
-    ada, b_ada_sum, b_down_sum, gain_one_sum, gain_two_sum, b_up_sum, times = results[11:18]
+    out_t, in_t, _, _, _, _, g_qkv, g_o, g_up, g_down, _, _ = results[:12]
+    ada, b_ada_sum, b_down_sum, gain_one_sum, gain_two_sum, b_up_sum, times = results[12:19]
     return (
         out_t.T,
         in_t.T,
         times,
-        jnp.swapaxes(g_heads[:3].astype(F32), 1, 2),
-        g_heads[3].astype(F32),
+        jnp.swapaxes(g_qkv.astype(F32), 1, 2),
+        g_o.astype(F32),
         g_up.astype(F32),
         b_up_sum,
         g_down.astype(F32),

time: 184 us -> 182 us (0.989)
    unnamed x31 -> x33, local copies, waits for them, and re-layouts: 7.59 us -> 6.84 us
where the time goes in v5:
time: 182 us; the launch traced here: 180 us
  Pallas kernels  166 us (91%)
  local copies, waits for them, and re-layouts  6.84 us (4%)
  other arithmetic  6.72 us (4%)
    pallas_call x1, Pallas kernels, layer(): pl.pallas_call(functools.partial(layer_kernel, n_wide, rows, width, size,...  166 us
    unnamed x33, local copies, waits for them, and re-layouts  6.84 us

profile of v5, /device:TPU:0, one launch (start us, length us, event | category | flops | bytes accessed | tf_op | source)
XLA Modules:
  0.0 180.3 jit_solution(14231559949966975877)
XLA Ops:
  0.7 166.0 %layer.1 = (bf16[192,1536]{1,0:T(8,128)(2,1)}, f32[192,1536]{1,0:T(8,128)}, bf16[4,384,128]{2,1,0:T(8,128)(2,1)}, bf16[4,384,128]{2,1,0:T(8,128)(2,1)}, bf16[4,1...) custom-call(s32[1,3]{1,0:T(1,128)} %refs_0_.1, ...), custom_call_target="tpu_custom_call" | custom-call | tf_op jit(solution)/shard_map/layer/pallas_call | solution.py:1372
  166.7 0.0 copy-start.1
  166.7 2.9 %convert_element_type.11 = f32[768,768]{1,0:T(8,128)} convert(bf16[768,768]{1,0:T(8,128)(2,1)} %get-tuple-element.31) | non-fusion elementwise | flops 589824 | bytes 3538944 | tf_op jit(solution)/shard_map/convert_element_type | solution.py:1415
  169.7 0.0 copy-done.1
  169.7 1.6 convert_element_type.12
  171.2 0.0 copy-done.3
  171.2 1.4 convert_bitcast_fusion
  172.6 0.0 copy-done.5
  172.6 0.9 convert_element_type.10
  173.5 0.0 copy-done.4
  173.5 0.8 copy.36
  174.3 0.0 copy-done.2
  174.3 0.0 copy-start
  174.3 1.0 copy.37
  175.3 0.0 copy-done.11
  175.3 0.6 copy.38
  175.9 0.0 copy-done.10
  175.9 0.6 copy.39
  176.5 0.6 copy.40
  177.1 0.6 copy.41
  177.7 0.6 copy.42
  178.3 0.0 copy-done
  178.3 1.4 copy.43
  179.7 0.6 copy.44
  (14 shorter events, 0.0 us)
Async XLA Ops:
  166.7 3.0 %copy-start.1 = (bf16[768,768]{1,0:T(8,128)(2,1)S(1)}, bf16[768,768]{1,0:T(8,128)(2,1)}, u32[]{:S(2)}) copy-start(bf16[768,768]{1,0:T(8,128)(2,1)} %get-tuple-element.33) | copy-start | bytes 3538948
  169.7 1.6 copy-start.3
  171.2 1.4 copy-start.5
  171.2 2.2 %copy-start.4 = (bf16[192,1536]{1,0:T(8,128)(2,1)S(1)}, bf16[192,1536]{1,0:T(8,128)(2,1)}, u32[]{:S(2)}) copy-start(bf16[192,1536]{1,0:T(8,128)(2,1)} %get-tuple-element.26) | copy-start | bytes 1769476
  172.6 1.7 copy-start.2
  173.5 1.9 %copy-start.11 = (f32[3,128]{1,0:T(4,128)S(1)}, f32[3,128]{1,0:T(4,128)}, u32[]{:S(2)}) copy-start(f32[3,128]{1,0:T(4,128)} %get-tuple-element.54) | copy-start | bytes 4612
  173.5 2.4 %copy-start.10 = (f32[768]{0:T(1024)S(1)}, f32[768]{0:T(1024)}, u32[]{:S(2)}) copy-start(f32[768]{0:T(1024)} %get-tuple-element.58) | copy-start | bytes 9220
  174.3 2.2 %copy-start.9 = (f32[768]{0:T(1024)S(1)}, f32[768]{0:T(1024)}, u32[]{:S(2)}) copy-start(f32[768]{0:T(1024)} %get-tuple-element.60) | copy-start | bytes 9220
  174.3 2.8 %copy-start.8 = (f32[768]{0:T(1024)S(1)}, f32[768]{0:T(1024)}, u32[]{:S(2)}) copy-start(f32[768]{0:T(1024)} %get-tuple-element.61) | copy-start | bytes 9220
  174.3 3.4 %copy-start.7 = (f32[768]{0:T(1024)S(1)}, f32[768]{0:T(1024)}, u32[]{:S(2)}) copy-start(f32[768]{0:T(1024)} %get-tuple-element.62) | copy-start | bytes 9220
  174.3 4.0 %copy-start = (f32[128,4608]{1,0:T(8,128)S(1)}, f32[128,4608]{1,0:T(8,128)}, u32[]{:S(2)}) copy-start(f32[128,4608]{1,0:T(8,128)} %get-tuple-element.63) | copy-start | bytes 7077892
  178.3 1.4 copy-start.6
